TPU v7x, 256 devices: a whole 4x4x8 slice. The times are simulated.
256 devices in a mesh: seq: 32 (over x, y, core), exp: 8 (over z).
Axes of the slice: x: 4, y: 4, z: 8, core: 2. Of those that a mesh axis runs over, the one named last changes fastest.
Arguments:
- tokens: bfloat16 [4096, 5120], P('seq', 'exp'), may hold values from -6 to 6
- out_grad: bfloat16 [4096, 5120], P('seq', 'exp'), may hold values from -0.59765625 to 0.59765625
- expert_ids: int32 [4096, 6], P('seq'), may hold values from 0 to 159, all different within a row; in each aligned block of 128 rows (0 to 127, 128 to 255, ...) at most 12 rows name the same one
- gates: bfloat16 [4096, 6], P('seq'), may hold values from 0.099609375 to 1
- w_gate: bfloat16 [32, 1536, 5120], P('seq', 'exp'), may hold values from -0.078125 to 0.078125
- w_up: bfloat16 [32, 1536, 5120], P('seq', 'exp'), may hold values from -0.078125 to 0.078125
- w_down: bfloat16 [32, 1536, 5120], P('seq', 'exp'), may hold values from -0.15625 to 0.15625
- shared_gate: bfloat16 [5120, 1536], P('seq', 'exp'), may hold values from -0.078125 to 0.078125
- shared_up: bfloat16 [5120, 1536], P('seq', 'exp'), may hold values from -0.078125 to 0.078125
- shared_down: bfloat16 [1536, 5120], P('exp', 'seq'), may hold values from -0.15625 to 0.15625
Outputs:
- token_grad: bfloat16 [4096, 5120], P('seq', 'exp')
- gate_grad: float32 [4096, 6], P('seq')
- grad_gate: bfloat16 [32, 1536, 5120], P('seq', 'exp')
- grad_up: bfloat16 [32, 1536, 5120], P('seq', 'exp')
- grad_down: bfloat16 [32, 1536, 5120], P('seq', 'exp')
- shared_grad_gate: bfloat16 [5120, 1536], P('seq', 'exp')
- shared_grad_up: bfloat16 [5120, 1536], P('seq', 'exp')
- shared_grad_down: bfloat16 [1536, 5120], P('exp', 'seq')
Inputs may be any that keep to these rules, and one draw needn't show every extreme that they name: `expert_ids`: in each aligned block of 128 rows (the tokens of one index of seq) no id is named by more than 12 rows. Ids of 32 or more name experts outside the window and take no part.
All inputs are finite; a program needn't handle non-finite values.
Results may differ from a plain program's by a relative error of at most 0.02.
Values may be sent and summed in bfloat16 or wider, within the bound.
A program may use at most 128 MiB of HBM per device.

v0:
```python
import jax
import jax.numpy as jnp
from jax import lax
from jax.sharding import PartitionSpec as P

TOPK = 6
MOST = 12


def dot_rows(left, right):
    return lax.dot_general(
        left, right, (((0,), (0,)), ((), ())), preferred_element_type=jnp.float32
    )


def dot_last(left, right):
    return lax.dot_general(
        left, right, (((1,), (1,)), ((), ())), preferred_element_type=jnp.float32
    )


def silu_parts(value):
    sig = jax.nn.sigmoid(value)
    return (value * sig, sig * (1.0 + value * (1.0 - sig)))


def body(
    tokens, out_grad, expert_ids, gates, w_gate, w_up, w_down, shared_gate, shared_up, shared_down
):
    num_seq = lax.axis_size("seq")
    tok_rows = tokens.shape[0]
    routes_here = tok_rows * TOPK
    dead = num_seq * MOST
    full_x, full_dy = (
        lax.all_gather(tokens, "exp", axis=1, tiled=True),
        lax.all_gather(out_grad, "exp", axis=1, tiled=True),
    )
    ids = expert_ids.reshape(-1)
    window = jnp.arange(num_seq, dtype=jnp.int32)
    onehot = (ids[:, None] == window[None, :]).astype(jnp.int32)
    rank = jnp.sum((jnp.cumsum(onehot, axis=0) - onehot) * onehot, axis=1)
    slot = jnp.where(ids < num_seq, ids * MOST + rank, dead)
    table = (
        jnp.full((dead + 1,), -1, jnp.int32)
        .at[slot]
        .set(jnp.arange(routes_here, dtype=jnp.int32))[:dead]
    )
    used = table >= 0
    safe = jnp.where(used, table, 0)
    token_of = safe // TOPK
    slot_gate = jnp.where(used, gates.reshape(-1)[safe], jnp.zeros((), jnp.bfloat16))
    send_x = jnp.where(used[:, None], tokens[token_of], jnp.zeros((), jnp.bfloat16))
    send_dy = jnp.where(used[:, None], out_grad[token_of], jnp.zeros((), jnp.bfloat16))
    part_x, part_dy, rows_gate = (
        lax.all_to_all(send_x, "seq", split_axis=0, concat_axis=0, tiled=True),
        lax.all_to_all(send_dy, "seq", split_axis=0, concat_axis=0, tiled=True),
        lax.all_to_all(slot_gate, "seq", split_axis=0, concat_axis=0, tiled=True),
    )
    rows_x, rows_dy = (
        lax.all_gather(part_x, "exp", axis=1, tiled=True),
        lax.all_gather(part_dy, "exp", axis=1, tiled=True),
    )
    weight_g = w_gate[0]
    weight_u = w_up[0]
    weight_d = w_down[0]
    weight = rows_gate.astype(jnp.float32)[:, None]
    pre_a = dot_last(rows_x, weight_g)
    pre_b = dot_last(rows_x, weight_u)
    act, slope = silu_parts(pre_a)
    hidden = act * pre_b
    back = dot_last(rows_dy, weight_d)
    dgate_part = jnp.sum(hidden * back, axis=1)
    scaled = weight * back
    grad_a = (scaled * pre_b * slope).astype(jnp.bfloat16)
    grad_b = (scaled * act).astype(jnp.bfloat16)
    hidden_w = (weight * hidden).astype(jnp.bfloat16)
    grad_down = dot_rows(hidden_w, rows_dy).astype(jnp.bfloat16)[None]
    grad_gate = dot_rows(grad_a, rows_x).astype(jnp.bfloat16)[None]
    grad_up = dot_rows(grad_b, rows_x).astype(jnp.bfloat16)[None]
    row_part = jnp.dot(grad_a, weight_g, preferred_element_type=jnp.float32) + jnp.dot(
        grad_b, weight_u, preferred_element_type=jnp.float32
    )
    row_sum = lax.psum_scatter(
        row_part.astype(jnp.bfloat16), "exp", scatter_dimension=1, tiled=True
    ).astype(jnp.float32)
    dgate_sum = lax.psum(dgate_part, "exp")
    back_rows, back_gate = (
        lax.all_to_all(
            row_sum.astype(jnp.bfloat16), "seq", split_axis=0, concat_axis=0, tiled=True
        ).astype(row_sum.dtype),
        lax.all_to_all(
            dgate_sum.astype(jnp.bfloat16), "seq", split_axis=0, concat_axis=0, tiled=True
        ).astype(dgate_sum.dtype),
    )
    padded_rows = jnp.concatenate(
        [back_rows, jnp.zeros((1, back_rows.shape[1]), jnp.float32)], axis=0
    )
    padded_gate = jnp.concatenate([back_gate, jnp.zeros((1,), jnp.float32)], axis=0)
    routed = jnp.sum(padded_rows[slot].reshape(tok_rows, TOPK, back_rows.shape[1]), axis=1)
    gate_grad = padded_gate[slot].reshape(tok_rows, TOPK)
    whole_g, whole_u, whole_d = (
        lax.all_gather(shared_gate, "seq", axis=0, tiled=True),
        lax.all_gather(shared_up, "seq", axis=0, tiled=True),
        lax.all_gather(shared_down, "seq", axis=1, tiled=True),
    )
    shared_a = jnp.dot(full_x, whole_g, preferred_element_type=jnp.float32)
    shared_b = jnp.dot(full_x, whole_u, preferred_element_type=jnp.float32)
    shared_act, shared_slope = silu_parts(shared_a)
    shared_back = dot_last(full_dy, whole_d)
    shared_da = (shared_back * shared_b * shared_slope).astype(jnp.bfloat16)
    shared_db = (shared_back * shared_act).astype(jnp.bfloat16)
    shared_hidden = (shared_act * shared_b).astype(jnp.bfloat16)
    part_g = dot_rows(full_x, shared_da)
    part_u = dot_rows(full_x, shared_db)
    part_d = dot_rows(shared_hidden, full_dy)
    sum_g, sum_u, sum_d = (
        lax.psum_scatter(
            part_g.astype(jnp.bfloat16), "seq", scatter_dimension=0, tiled=True
        ).astype(jnp.float32),
        lax.psum_scatter(
            part_u.astype(jnp.bfloat16), "seq", scatter_dimension=0, tiled=True
        ).astype(jnp.float32),
        lax.psum_scatter(
            part_d.astype(jnp.bfloat16), "seq", scatter_dimension=1, tiled=True
        ).astype(jnp.float32),
    )
    shared_part = dot_last(shared_da, whole_g) + dot_last(shared_db, whole_u)
    shared_rows = lax.psum_scatter(
        shared_part.astype(jnp.bfloat16), "exp", scatter_dimension=1, tiled=True
    ).astype(jnp.float32)
    token_grad = (routed + shared_rows).astype(jnp.bfloat16)
    return (
        token_grad,
        gate_grad,
        grad_gate,
        grad_up,
        grad_down,
        sum_g.astype(jnp.bfloat16),
        sum_u.astype(jnp.bfloat16),
        sum_d.astype(jnp.bfloat16),
    )


def solution(mesh):
    return jax.shard_map(
        body,
        mesh=mesh,
        in_specs=(
            P("seq", "exp"),
            P("seq", "exp"),
            P("seq", None),
            P("seq", None),
            P("seq", "exp", None),
            P("seq", "exp", None),
            P("seq", "exp", None),
            P("seq", "exp"),
            P("seq", "exp"),
            P("exp", "seq"),
        ),
        out_specs=(
            P("seq", "exp"),
            P("seq", None),
            P("seq", "exp", None),
            P("seq", "exp", None),
            P("seq", "exp", None),
            P("seq", "exp"),
            P("seq", "exp"),
            P("exp", "seq"),
        ),
        check_vma=False,
    )
```

profile of v0, /device:TPU:1, one launch (start us, length us, event | category | flops | bytes accessed | tf_op | source)
XLA Modules:
  0.0 725.3 jit_solution(6158549614565875271)
XLA Ops:
  13.7 1.7 reduce-window.6
  15.8 3.4 scatter_custom_fusion
  19.4 2.6 gather_fusion.2
  22.0 2.6 gather_fusion.1
  25.8 2.0 gather.21
  27.8 1.3 broadcast_select_fusion.1
  29.1 21.3 %all_to_all.43 = bf16[32,12,640]{2,1,0:T(8,128)(2,1)S(1)} all-to-all(bf16[32,12,640]{2,1,0:T(8,128)(2,1)S(1)} %get-tuple-element.40), channel_id=1, replica_groups=mesh['seq'=32,'exp'=8] {'seq'}, dimensions={0} | all-to-all | bytes 983040 | tf_op jit(solution)/shard_map/all_to_all | solution.py:55
  51.4 16.5 %all_to_all.44 = bf16[32,12,640]{2,1,0:T(8,128)(2,1)S(1)} all-to-all(bf16[32,12,640]{2,1,0:T(8,128)(2,1)S(1)} %get-tuple-element.39), channel_id=1, replica_groups=mesh['seq'=32,'exp'=8] {'seq'}, dimensions={0} | all-to-all | bytes 983040 | tf_op jit(solution)/shard_map/all_to_all | solution.py:56
  69.1 2.8 gather_fusion
  72.0 31.9 %all-gather.20.cloned.1.call-done = bf16[5120,192]{1,0:T(8,128)(2,1)} async-done(((bf16[160,192]{1,0:T(8,128)(2,1)}), bf16[5120,192]{1,0:T(8,128)(2,1)}) %all-gather.20.cloned.1.call-update) | async-done | bytes 1966096 | tf_op jit(solution)/shard_map/all_gather | solution.py:102
  104.0 3.2 fusion.31
  107.1 48.3 %all-gather.18.cloned.1.call-done = bf16[5120,192]{1,0:T(8,128)(2,1)} async-done(((bf16[160,192]{1,0:T(8,128)(2,1)}), bf16[5120,192]{1,0:T(8,128)(2,1)}) %all-gather.18.cloned.1.call-update) | async-done | bytes 1966096 | tf_op jit(solution)/shard_map/all_gather | solution.py:103
  155.5 2.8 fusion.30
  158.2 32.7 %all-gather.12.cloned.1.call-done = bf16[128,5120]{1,0:T(8,128)(2,1)} async-done(((bf16[128,640]{1,0:T(8,128)(2,1)}), bf16[128,5120]{1,0:T(8,128)(2,1)}) %all-gather.12.cloned.1.call-update) | async-done | bytes 1310736 | tf_op jit(solution)/shard_map/all_gather | solution.py:36
  191.0 55.3 %all-gather.14.cloned.1.call-done = bf16[192,5120]{0,1:T(8,128)(2,1)} async-done(((bf16[192,160]{0,1:T(8,128)(2,1)}), bf16[192,5120]{0,1:T(8,128)(2,1)}) %all-gather.14.cloned.1.call-update) | async-done | bytes 1966096 | tf_op jit(solution)/shard_map/all_gather | solution.py:104
  246.3 3.3 multiply_convert_fusion.5
  251.4 2.1 fusion
  253.5 2.4 copy.42
  256.1 12.0 %all_to_all.45 = bf16[32,12,1]{1,2,0:T(2,128)(2,1)S(1)} all-to-all(bf16[32,12,1]{1,2,0:T(2,128)(2,1)S(1)} %select_n.72), channel_id=1, replica_groups=mesh['seq'=32,'exp'=8] {'seq'}, dimensions={0} | all-to-all | bytes 1536 | tf_op jit(solution)/shard_map/all_to_all | solution.py:57
  268.2 31.7 %all-gather.10.cloned.1.call-done = bf16[384,5120]{1,0:T(8,128)(2,1)} async-done(((bf16[384,640]{1,0:T(8,128)(2,1)}), bf16[384,5120]{1,0:T(8,128)(2,1)}) %all-gather.10.cloned.1.call-update) | async-done | bytes 3932176 | tf_op jit(solution)/shard_map/all_gather | solution.py:60
  299.9 4.4 fusion.8
  304.4 2.2 fusion.11
  306.6 46.2 %all-gather.8.cloned.1.call-done = bf16[384,5120]{1,0:T(8,128)(2,1)} async-done(((bf16[384,640]{1,0:T(8,128)(2,1)}), bf16[384,5120]{1,0:T(8,128)(2,1)}) %all-gather.8.cloned.1.call-update) | async-done | bytes 3932176 | tf_op jit(solution)/shard_map/all_gather | solution.py:61
  352.7 4.3 multiply_reduce_fusion
  357.1 1.2 fusion.6
  358.7 3.2 add_convert_fusion
  361.9 6.2 copy.40
  368.2 1.2 copy-done.8
  369.4 2.4 convolution_convert_fusion
  371.9 1.5 fusion.1
  373.4 2.6 copy.44
  376.7 2.6 copy.46
  379.2 10.5 %reduce-scatter.18.cloned.1.call-done = bf16[640,128]{1,0:T(8,128)(2,1)} async-done(((bf16[5120,128]{1,0:T(8,128)(2,1)}), bf16[640,128]{1,0:T(8,128)(2,1)}) %reduce-scatter.18.cloned.1.call-update) | async-done | bytes 163856
  390.8 12.1 %psum.7 = bf16[384]{0:T(512)(128)(2,1)S(1)} all-reduce(f32[384]{0:T(512)S(1)} %get-tuple-element.34), channel_id=1, replica_groups=mesh['seq'=32,'exp'=8] {'exp'}, use_global_device_ids=true, to_apply=%region_8.9 | all-reduce | flops 384 | bytes 2304 | tf_op jit(solution)/shard_map/psum | solution.py:86
  403.7 15.1 %all-to-all-start.4 = ((bf16[32,12,1]{1,2,0:T(2,128)(2,1)}), bf16[32,12,1]{1,2,0:T(2,128)(2,1)S(1)}, u32[]{:S(2)}, u32[]{:S(2)}) async-start(bf16[32,12,1]{1,2,0:T(2,128)(2,1)} %all_to_all.37), calls=%async_computation.4 | async-start | bytes 32768 | tf_op jit(solution)/shard_map/all_to_all | solution.py:91
  418.8 4.6 fusion.3
  423.5 24.6 %reduce-scatter.16.cloned.1.call-done = bf16[640,384]{1,0:T(8,128)(2,1)} async-done(((bf16[5120,384]{1,0:T(8,128)(2,1)}), bf16[640,384]{1,0:T(8,128)(2,1)}) %reduce-scatter.16.cloned.1.call-update) | async-done | bytes 491536
  448.0 1.3 copy.41
  450.3 7.5 %all-to-all-start.3 = ((bf16[32,12,640]{2,1,0:T(8,128)(2,1)}), bf16[32,12,640]{2,1,0:T(8,128)(2,1)S(1)}, u32[]{:S(2)}, u32[]{:S(2)}) async-start(bf16[32,12,640]{2,1,0:T(8,128)(2,1)} %all_to_all.33), calls=%async_computation.3 | async-start | bytes 1310720 | tf_op jit(solution)/shard_map/all_to_all | solution.py:88
  457.9 4.7 fusion.4
  462.6 2.5 fusion.5
  465.3 5.0 gather_fusion.4
  471.3 3.4 gather_fusion.3
  474.7 3.2 reshape.147
  477.9 2.6 reduce_sum.31
  481.2 55.2 %reduce-scatter.14.cloned.1.call-done = bf16[192,160]{0,1:T(8,128)(2,1)} async-done(((bf16[192,5120]{0,1:T(8,128)(2,1)}), bf16[192,160]{0,1:T(8,128)(2,1)}) %reduce-scatter.14.cloned.1.call-update) | async-done | bytes 61456 | tf_op jit(solution)/shard_map/reduce_scatter | solution.py:123
  536.4 91.4 %reduce-scatter.20.cloned.1.call-done = bf16[160,192]{1,0:T(8,128)(2,1)} async-done(((bf16[5120,192]{1,0:T(8,128)(2,1)}), bf16[160,192]{1,0:T(8,128)(2,1)}) %reduce-scatter.20.cloned.1.call-update) | async-done | bytes 61456
  627.8 90.7 %reduce-scatter.22.cloned.1.call-done = bf16[160,192]{1,0:T(8,128)(2,1)} async-done(((bf16[5120,192]{1,0:T(8,128)(2,1)}), bf16[160,192]{1,0:T(8,128)(2,1)}) %reduce-scatter.22.cloned.1.call-update) | async-done | bytes 61456
  (109 shorter events, 18.4 us)
Async XLA Ops:
  7.2 292.8 %copy-start = (bf16[1,192,5120]{2,1,0:T(8,128)(2,1)S(1)}, bf16[1,192,5120]{2,1,0:T(8,128)(2,1)}, u32[]{:S(2)}) copy-start(bf16[1,192,5120]{2,1,0:T(8,128)(2,1)} %param.14) | copy-start | bytes 5898244
  7.2 12.2 %copy-start.2 = (bf16[128,640]{1,0:T(8,128)(2,1)S(1)}, bf16[128,640]{1,0:T(8,128)(2,1)}, u32[]{:S(2)}) copy-start(bf16[128,640]{1,0:T(8,128)(2,1)} %param.10) | copy-start | bytes 491524
  7.2 64.8 %all-gather.16.cloned.1.call-start = ((), (), s32[]{:S(2)}) async-start(), calls=%async_computation.14 | async-start | bytes 1474560 | tf_op jit(solution)/shard_map/all_gather | solution.py:35
  7.9 96.0 %all-gather.20.cloned.1.call-start = ((), (), s32[]{:S(2)}) async-start(), calls=%async_computation.16 | async-start | bytes 2703360 | tf_op jit(solution)/shard_map/all_gather | solution.py:102
  8.7 146.8 %all-gather.18.cloned.1.call-start = ((), (), s32[]{:S(2)}) async-start(), calls=%async_computation.15 | async-start | bytes 2703360 | tf_op jit(solution)/shard_map/all_gather | solution.py:103
  9.4 181.6 %all-gather.12.cloned.1.call-start = ((), (), s32[]{:S(2)}) async-start(), calls=%async_computation.12 | async-start | bytes 1474560 | tf_op jit(solution)/shard_map/all_gather | solution.py:36
  10.0 236.3 %all-gather.14.cloned.1.call-start = ((), (), s32[]{:S(2)}) async-start(), calls=%async_computation.13 | async-start | bytes 2703360 | tf_op jit(solution)/shard_map/all_gather | solution.py:104
  10.6 289.4 %all-gather.10.cloned.1.call-start = ((), (), s32[]{:S(2)}) async-start(), calls=%async_computation.11 | async-start | bytes 4423680 | tf_op jit(solution)/shard_map/all_gather | solution.py:60
  11.6 10.5 %copy-start.3 = (bf16[128,640]{1,0:T(8,128)(2,1)S(1)}, bf16[128,640]{1,0:T(8,128)(2,1)}, u32[]{:S(2)}) copy-start(bf16[128,640]{1,0:T(8,128)(2,1)} %param.11) | copy-start | bytes 491524
  50.4 18.4 %copy-start.19 = (bf16[128,6]{0,1:T(8,128)(2,1)S(1)}, bf16[128,6]{0,1:T(8,128)(2,1)}, u32[]{:S(2)}) copy-start(bf16[128,6]{0,1:T(8,128)(2,1)} %param.13) | copy-start | bytes 4612
  51.4 301.4 %all-gather.8.cloned.1.call-start = ((), (), s32[]{:S(2)}) async-start(), calls=%async_computation.10 | async-start | bytes 4423680 | tf_op jit(solution)/shard_map/all_gather | solution.py:61
  68.8 321.0 %reduce-scatter.18.cloned.1.call-start = ((), (), s32[]{:S(2)}) async-start(), calls=%async_computation.19 | async-start | bytes 1474560
  72.0 83.5 %copy-start.5 = (bf16[128,5120]{1,0:T(8,128)(2,1)S(1)}, bf16[128,5120]{1,0:T(8,128)(2,1)}, u32[]{:S(2)}) copy-start(bf16[128,5120]{1,0:T(8,128)(2,1)} %all-gather.16.cloned.1.call-done) | copy-start | bytes 3932164
  246.3 3.3 copy-start.6
  249.6 1.0 copy-start.16
  249.6 1.8 copy-start.7
  255.9 192.1 %reduce-scatter.16.cloned.1.call-start = ((), (), s32[]{:S(2)}) async-start(), calls=%async_computation.18 | async-start | bytes 4423680
  299.9 4.4 copy-start.4
  299.9 4.4 copy-start.10
  357.0 1.3 copy-start.14
  357.0 1.3 copy-start.12
  357.1 1.7 copy-start.11
  368.1 1.3 copy-start.8
  368.1 168.3 %reduce-scatter.14.cloned.1.call-start = ((), (), s32[]{:S(2)}) async-start(), calls=%async_computation.17 | async-start | bytes 2703360 | tf_op jit(solution)/shard_map/reduce_scatter | solution.py:123
  371.8 256.0 %reduce-scatter.20.cloned.1.call-start = ((), (), s32[]{:S(2)}) async-start(), calls=%async_computation.20 | async-start | bytes 2703360
  375.9 342.6 %reduce-scatter.22.cloned.1.call-start = ((), (), s32[]{:S(2)}) async-start(), calls=%async_computation.21 | async-start | bytes 2703360
  379.2 39.6 %copy-start.15 = (bf16[384,192]{0,1:T(8,128)(2,1)S(1)}, bf16[384,192]{0,1:T(8,128)(2,1)}, u32[]{:S(2)}) copy-start(bf16[384,192]{0,1:T(8,128)(2,1)} %copy-done.14) | copy-start | bytes 442372
  403.7 46.6 %all-to-all-start.4 = ((bf16[32,12,1]{1,2,0:T(2,128)(2,1)}), bf16[32,12,1]{1,2,0:T(2,128)(2,1)S(1)}, u32[]{:S(2)}, u32[]{:S(2)}) async-start(bf16[32,12,1]{1,2,0:T(2,128)(2,1)} %all_to_all.37), calls=%async_computation.4 | async-start | bytes 32768 | tf_op jit(solution)/shard_map/all_to_all | solution.py:91
  423.5 34.4 %copy-start.13 = (bf16[384,192]{0,1:T(8,128)(2,1)S(1)}, bf16[384,192]{0,1:T(8,128)(2,1)}, u32[]{:S(2)}) copy-start(bf16[384,192]{0,1:T(8,128)(2,1)} %copy-done.12) | copy-start | bytes 442372
  450.3 20.8 %all-to-all-start.3 = ((bf16[32,12,640]{2,1,0:T(8,128)(2,1)}), bf16[32,12,640]{2,1,0:T(8,128)(2,1)S(1)}, u32[]{:S(2)}, u32[]{:S(2)}) async-start(bf16[32,12,640]{2,1,0:T(8,128)(2,1)} %all_to_all.33), calls=%async_computation.3 | async-start | bytes 1310720 | tf_op jit(solution)/shard_map/all_to_all | solution.py:88
  457.8 4.8 copy-start.9
  457.8 4.8 copy-start.17
  457.8 4.8 copy-start.18
  474.7 243.8 %copy-start.1 = (bf16[1,192,5120]{2,1,0:T(8,128)(2,1)S(1)}, bf16[1,192,5120]{2,1,0:T(8,128)(2,1)}, u32[]{:S(2)}) copy-start(bf16[1,192,5120]{2,1,0:T(8,128)(2,1)} %param.14) | copy-start | bytes 5898244
Sparse Core Ops, SparseCore 0:
  9.8 38.7 all-gather.15
  51.2 52.7 all-gather.19
  106.5 48.9 all-gather.17
  157.1 33.8 all-gather.11
  193.4 52.8 all-gather.13
  248.5 51.3 all-gather.9
  301.7 50.9 all-gather.7
  355.8 33.8 reduce-scatter.17
  392.3 55.6 reduce-scatter.15
  452.3 84.0 reduce-scatter.13
  541.3 86.4 reduce-scatter.19
  632.1 86.3 reduce-scatter.21
where the time goes:
time: 727 us; the launch traced here: 725 us
  waiting for transfers between devices  522 us (72%)
  blocking collectives  61.9 us (9%)
  local copies, waits for them, and re-layouts  51.8 us (7%)
  matrix products  44 us (6%)
  starting transfers between devices  23.1 us (3%)
  between operations  14.6 us (2%)
  other arithmetic  8.09 us (1%)
    unnamed x16, waiting for transfers between devices  220 us
    all_gather x1, waiting for transfers between devices, body(): lax.all_gather(shared_down, 'seq', axis=1, tiled=True)  55.3 us
    reduce_scatter x1, waiting for transfers between devices, body(): lax.psum_scatter(part_d.astype(jnp.bfloat16), 'seq', scatter_dimension=1,...  55.2 us
    all_gather x1, waiting for transfers between devices, body(): lax.all_gather(shared_up, 'seq', axis=0, tiled=True)  48.3 us
    all_gather x1, waiting for transfers between devices, body(): lax.all_gather(part_dy, 'exp', axis=1, tiled=True)  46.2 us
    all_gather x1, waiting for transfers between devices, body(): lax.all_gather(out_grad, 'exp', axis=1, tiled=True)  32.7 us
    all_gather x1, waiting for transfers between devices, body(): lax.all_gather(shared_gate, 'seq', axis=0, tiled=True)  31.9 us
    all_gather x1, waiting for transfers between devices, body(): lax.all_gather(part_x, 'exp', axis=1, tiled=True)  31.7 us
  transfers between devices with their start and end apart: 14, of which 11 were waited for; matrix products, arithmetic and copies ran while one was open for 13% of the time, Pallas kernels for 0%

commit v1 on v0

v1 whole, which is shorter than its diff:
```python
import functools

import jax
import jax.numpy as jnp
from jax import lax
from jax.experimental import pallas as pl
from jax.experimental.pallas import tpu as pltpu
from jax.sharding import PartitionSpec as P

MESH = pl.DeviceIdType.MESH
MOST = 12
SLOT = 16
SIDE = 4
BLOCK = 128
MIB = 1 << 20
F32 = jnp.float32
BF16 = jnp.bfloat16


def dot(left, right):
    return jnp.dot(left, right, preferred_element_type=F32)


def dot_last(left, right):
    return lax.dot_general(left, right, (((1,), (1,)), ((), ())), preferred_element_type=F32)


def dot_rows(left, right):
    return lax.dot_general(left, right, (((0,), (0,)), ((), ())), preferred_element_type=F32)


def silu_parts(value):
    sig = jax.nn.sigmoid(value)
    return value * sig, sig * (1.0 + value * (1.0 - sig))


def ring(value, size):
    return lax.rem(value + size, size)


def place():
    seq, exp = lax.axis_index("seq"), lax.axis_index("exp")
    return (
        seq,
        exp,
        lax.div(seq, 2 * SIDE),
        lax.rem(lax.div(seq, 2), SIDE),
        lax.rem(seq, 2),
    )


def remote(src, dst, send_sem, recv_sem, device):
    return pltpu.make_async_remote_copy(
        src_ref=src,
        dst_ref=dst,
        send_sem=send_sem,
        recv_sem=recv_sem,
        device_id=device,
        device_id_type=MESH,
    )


def greet(barrier, device):
    pl.semaphore_signal(barrier, inc=1, device_id=device, device_id_type=MESH)


def has_step(step, way, sub):
    return step < 4 or way == sub


class ZRing:
    def __init__(self, own, bufs, seq, exp, send_sem, recv_sem):
        self.own, self.bufs, self.seq, self.exp = own, bufs, seq, exp
        self.send_sem, self.recv_sem = send_sem, recv_sem

    def copy(self, step, way, sub, landed=False):
        sign = 1 - 2 * way
        piece = ring(self.exp - sign * (step if landed else step - 1), 8)
        slot = self.bufs[sub].at[piece]
        src = self.own[sub] if step == 1 and not landed else slot
        return remote(
            src,
            slot,
            self.send_sem.at[way, sub, step - 1],
            self.recv_sem.at[way, sub, step - 1],
            (self.seq, ring(self.exp + sign, 8)),
        )

    def start(self, step):
        for sub in range(2):
            for way in range(2):
                if has_step(step, way, sub):
                    self.copy(step, way, sub).start()

    def land(self, step):
        for sub in range(2):
            for way in range(2):
                if has_step(step, way, sub):
                    self.copy(step, way, sub, landed=True).wait_recv()
                    if step < 4 and has_step(step + 1, way, sub):
                        self.copy(step + 1, way, sub).start()

    def finish(self):
        for step in range(1, 5):
            for sub in range(2):
                for way in range(2):
                    if has_step(step, way, sub):
                        self.copy(step, way, sub).wait_send()


class Plane:
    def __init__(self):
        self.seq, self.exp, self.x, self.y, self.core = place()

    def device(self, along_x, step):
        x = ring(self.x + step, SIDE) if along_x else self.x
        y = self.y if along_x else ring(self.y + step, SIDE)
        return ((x * SIDE + y) * 2 + self.core, self.exp)

    def view(self, ref, half, wide, along_x, step):
        count = ref.shape[3] // 2
        rows = pl.ds(half * count, count)
        here = ring((self.x if along_x else self.y) + step, SIDE)
        if along_x:
            return ref.at[here, :, self.core, rows] if wide else ref.at[here, self.y, self.core, rows]
        return ref.at[:, here, self.core, rows] if wide else ref.at[self.x, here, self.core, rows]


def spread_kernel(
    send, tok, grad, shared, rows_o, tok_o, grad_o, shared_o, own_sem, a_s, a_r, z_s, z_r, w_s, w_r, b_s, b_r
):
    plane = Plane()
    seq, exp, core = plane.seq, plane.exp, plane.core
    sibling = (seq + 1 - 2 * core, exp)
    own = [
        pltpu.make_async_copy(send.at[seq], rows_o.at[seq], own_sem.at[0]),
        pltpu.make_async_copy(tok, tok_o.at[exp], own_sem.at[1]),
        pltpu.make_async_copy(grad, grad_o.at[exp], own_sem.at[2]),
        pltpu.make_async_copy(shared, shared_o.at[plane.x, plane.y, core], own_sem.at[3]),
    ]
    for copy in own:
        copy.start()
    barrier = pltpu.get_barrier_semaphore()

    def hello(step, carry):
        greet(barrier, (ring(seq + step, 32), exp))
        return carry

    lax.fori_loop(1, 32, hello, 0)
    greet(barrier, (seq, ring(exp + 1, 8)))
    greet(barrier, (seq, ring(exp - 1, 8)))
    pl.semaphore_wait(barrier, 33)

    tokens = ZRing((tok, grad), (tok_o, grad_o), seq, exp, z_s, z_r)
    tokens.start(1)

    def exchange(step, landed):
        to, source = ring(seq + step, 32), ring(seq - step, 32)
        return remote(
            send.at[to],
            rows_o.at[source if landed else seq],
            a_s.at[step - 1],
            a_r.at[step - 1],
            (to, exp),
        )

    def exchange_start(step, carry):
        exchange(step, False).start()
        return carry

    lax.fori_loop(1, 32, exchange_start, 0)
    own[3].wait()

    def weight(half, phase, kind, landed):
        along_x = half != phase
        sign = 1 - 2 * half
        wide = phase == 1
        if kind == 0:
            to, piece = sign, (-sign if landed else 0)
        elif kind == 1:
            to, piece = -sign, (sign if landed else 0)
        else:
            to, piece = sign, (2 if landed else -sign)
        part = plane.view(shared_o, half, wide, along_x, piece)
        return remote(
            part, part, w_s.at[half, phase, kind], w_r.at[half, phase, kind], plane.device(along_x, to)
        )

    def across(half, phase, index, landed):
        along_x = half != phase
        sign = 1 - 2 * half
        wide = phase == 1
        piece = (0, -sign, sign, 2)[index]
        core_here = plane.core
        if landed:
            plane.core = 1 - core_here
        part = plane.view(shared_o, half, wide, along_x, piece)
        plane.core = core_here
        return remote(part, part, b_s.at[half, phase, index], b_r.at[half, phase, index], sibling)

    for half in range(2):
        weight(half, 0, 0, False).start()
        weight(half, 0, 1, False).start()
        across(half, 0, 0, False).start()

    def weight_near(phase):
        for half in range(2):
            weight(half, phase, 0, True).wait_recv()
            weight(half, phase, 2, False).start()
            across(half, phase, 1, False).start()
            weight(half, phase, 1, True).wait_recv()
            across(half, phase, 2, False).start()

    def weight_far(phase):
        for half in range(2):
            weight(half, phase, 2, True).wait_recv()
            if phase == 0:
                weight(half, 1, 0, False).start()
                weight(half, 1, 1, False).start()
            across(half, phase, 3, False).start()

    weight_near(0)
    weight_far(0)
    tokens.land(1)
    weight_near(1)
    tokens.land(2)
    weight_far(1)
    tokens.land(3)
    tokens.land(4)

    def exchange_end(step, carry):
        exchange(step, True).wait_recv()
        exchange(step, False).wait_send()
        return carry

    lax.fori_loop(1, 32, exchange_end, 0)
    for copy in own[:3]:
        copy.wait()
    tokens.finish()
    for half in range(2):
        for phase in range(2):
            for kind in range(3):
                weight(half, phase, kind, False).wait_send()
            for index in range(1 if phase else 0, 4):
                across(half, phase, index, True).wait_recv()
                across(half, phase, index, False).wait_send()


def any_specs(count):
    return [pl.BlockSpec(memory_space=pl.ANY)] * count


def vmem_specs(count):
    return [pl.BlockSpec(memory_space=pltpu.VMEM)] * count


def spread(send, tok, grad, shared):
    rows, width = tok.shape
    dma = pltpu.SemaphoreType.DMA
    return pl.pallas_call(
        spread_kernel,
        out_shape=(
            jax.ShapeDtypeStruct(send.shape, BF16),
            jax.ShapeDtypeStruct((8, rows, width), BF16),
            jax.ShapeDtypeStruct((8, rows, width), BF16),
            jax.ShapeDtypeStruct((SIDE, SIDE, 2) + shared.shape, BF16),
        ),
        in_specs=any_specs(4),
        out_specs=any_specs(4),
        scratch_shapes=[
            dma((4,)),
            dma((31,)),
            dma((31,)),
            dma((2, 2, 4)),
            dma((2, 2, 4)),
            dma((2, 2, 3)),
            dma((2, 2, 3)),
            dma((2, 2, 4)),
            dma((2, 2, 4)),
        ],
        compiler_params=pltpu.CompilerParams(collective_id=0, has_side_effects=True),
    )(send, tok, grad, shared)


def back_kernel(send, rows_o, own_sem, a_s, a_r):
    seq, exp = lax.axis_index("seq"), lax.axis_index("exp")
    own = pltpu.make_async_copy(send.at[seq], rows_o.at[seq], own_sem)
    own.start()
    barrier = pltpu.get_barrier_semaphore()

    def hello(step, carry):
        greet(barrier, (ring(seq + step, 32), exp))
        return carry

    lax.fori_loop(1, 32, hello, 0)
    pl.semaphore_wait(barrier, 31)

    def exchange(step, landed):
        to, source = ring(seq + step, 32), ring(seq - step, 32)
        return remote(
            send.at[to],
            rows_o.at[source if landed else seq],
            a_s.at[step - 1],
            a_r.at[step - 1],
            (to, exp),
        )

    def exchange_start(step, carry):
        exchange(step, False).start()
        return carry

    def exchange_end(step, carry):
        exchange(step, True).wait_recv()
        exchange(step, False).wait_send()
        return carry

    lax.fori_loop(1, 32, exchange_start, 0)
    lax.fori_loop(1, 32, exchange_end, 0)
    own.wait()


def send_back(send):
    dma = pltpu.SemaphoreType.DMA
    return pl.pallas_call(
        back_kernel,
        out_shape=jax.ShapeDtypeStruct(send.shape, BF16),
        in_specs=vmem_specs(1),
        out_specs=vmem_specs(1)[0],
        scratch_shapes=[dma, dma((31,)), dma((31,))],
        compiler_params=pltpu.CompilerParams(collective_id=3, has_side_effects=True),
    )(send)


def expert_kernel(
    row_x, row_y, gate, w_gate, w_up, w_down, tok, grad, shared,
    row_sum, shared_rows, out_gate, out_up, out_down, out_shared,
    xb, yb, wg, wu, wd, tx, ty, ws,
    s_acc, s_dab, s_h, gp, sib, qa, qb,
    acc_a, acc_b, acc_u, da, db, hw, dat, dbt, hwt, dg,
    pb, rp, rm, stage,
    own_sem, z_s, z_r, c_s, c_r, q_s, q_r, p_s, p_r, o_s,
):
    plane = Plane()
    seq, exp, core = plane.seq, plane.exp, plane.core
    sibling = (seq + 1 - 2 * core, exp)
    count, width = row_x.shape
    tok_rows = tok.shape[1]
    total = count + 16 + tok_rows
    split = -(-total // 32) * 16
    lanes = ws.shape[2] // 3

    own = [
        pltpu.make_async_copy(src, dst, own_sem.at[i])
        for i, (src, dst) in enumerate(
            (
                (tok, tx),
                (grad, ty),
                (shared, ws),
                (row_x, xb.at[exp]),
                (row_y, yb.at[exp]),
                (w_gate, wg),
                (w_up, wu),
                (w_down, wd),
            )
        )
    ]
    for copy in own:
        copy.start()
    barrier = pltpu.get_barrier_semaphore()
    greet(barrier, (seq, ring(exp + 1, 8)))
    greet(barrier, (seq, ring(exp - 1, 8)))
    greet(barrier, plane.device(True, 1))
    greet(barrier, plane.device(True, -1))
    greet(barrier, plane.device(False, 1))
    greet(barrier, plane.device(False, -1))
    greet(barrier, sibling)
    pl.semaphore_wait(barrier, 7)

    rows = ZRing((row_x, row_y), (xb, yb), seq, exp, z_s, z_r)
    rows.start(1)

    for copy in own[:3]:
        copy.wait()
    s_acc[...] = jnp.zeros_like(s_acc)

    def shared_forward(piece, carry):
        s_acc[:, : 2 * lanes] += dot(tx[piece], ws[piece, :, : 2 * lanes])
        s_acc[:, 2 * lanes :] += dot(ty[piece], ws[piece, :, 2 * lanes :])
        return carry

    lax.fori_loop(0, 8, shared_forward, 0)
    act, slope = silu_parts(s_acc[:, :lanes])
    up, back = s_acc[:, lanes : 2 * lanes], s_acc[:, 2 * lanes :]
    s_dab[:, :lanes] = (back * up * slope).astype(BF16)
    s_dab[:, lanes:] = (back * act).astype(BF16)
    s_h[...] = (act * up).astype(BF16)

    def shared_grads(piece, carry):
        at_x, at_y = lax.div(piece, 2), 2 * lax.rem(piece, 2)
        part = dot_rows(tx[piece], s_dab[...]).astype(BF16)
        gp[at_x, pl.ds(at_y, 2), :, :, : 2 * lanes] = part.reshape(2, 2, width // 4, 2 * lanes)
        part = dot_rows(ty[piece], s_h[...]).astype(BF16)
        gp[at_x, pl.ds(at_y, 2), :, :, 2 * lanes :] = part.reshape(2, 2, width // 4, lanes)
        return carry

    lax.fori_loop(0, 8, shared_grads, 0)
    across = remote(gp.at[:, :, 1 - core], sib, c_s, c_r, sibling)
    across.start()

    for copy in own[3:]:
        copy.wait()
    acc_a[...] = jnp.zeros_like(acc_a)
    acc_b[...] = jnp.zeros_like(acc_b)
    acc_u[...] = jnp.zeros_like(acc_u)

    def forward(piece):
        cols = pl.ds(pl.multiple_of(piece * width, 128), width)

        def block(index, carry):
            at = pl.ds(pl.multiple_of(index * BLOCK, BLOCK), BLOCK)
            acc_a[at] += dot_last(xb[piece, at], wg[:, cols])
            acc_b[at] += dot_last(xb[piece, at], wu[:, cols])
            acc_u[at] += dot_last(yb[piece, at], wd[:, cols])
            return carry

        lax.fori_loop(0, count // BLOCK, block, 0)

    forward(exp)

    def landing(half, phase, kind):
        return qb.at[half, kind] if phase else qa.at[half, kind]

    def reduce_copy(half, phase, kind):
        along_x = half == phase
        sign = 1 - 2 * half
        piece, to = ((2, sign), (-sign, -sign), (sign, sign))[kind]
        return remote(
            plane.view(gp, half, phase == 0, along_x, piece),
            landing(half, phase, kind),
            q_s.at[half, phase, kind],
            q_r.at[half, phase, kind],
            plane.device(along_x, to),
        )

    def reduce_add(half, phase, step, kinds):
        mine = plane.view(gp, half, phase == 0, half == phase, step)
        value = mine[...].astype(F32)
        for kind in kinds:
            value += landing(half, phase, kind)[...].astype(F32)
        mine[...] = value.astype(BF16)

    def reduce_start(phase):
        for half in range(2):
            reduce_copy(half, phase, 0).start()
            reduce_copy(half, phase, 1).start()

    def reduce_pass(phase):
        for half in range(2):
            reduce_copy(half, phase, 0).wait_recv()
            reduce_add(half, phase, 1 - 2 * half, (0,))
            reduce_copy(half, phase, 2).start()

    def reduce_end(phase):
        for half in range(2):
            reduce_copy(half, phase, 1).wait_recv()
            reduce_copy(half, phase, 2).wait_recv()
            reduce_add(half, phase, 0, (1, 2))

    across.wait_recv()

    def add_sibling(index, carry):
        at_x, at_y = lax.div(index, SIDE), lax.rem(index, SIDE)
        gp[at_x, at_y, core] = (
            gp[at_x, at_y, core].astype(F32) + sib[at_x, at_y].astype(F32)
        ).astype(BF16)
        return carry

    lax.fori_loop(0, SIDE * SIDE, add_sibling, 0)
    reduce_start(0)

    rows.land(1)
    forward(ring(exp - 1, 8))
    forward(ring(exp + 1, 8))
    reduce_pass(0)
    rows.land(2)
    forward(ring(exp - 2, 8))
    forward(ring(exp + 2, 8))
    reduce_end(0)
    reduce_start(1)
    rows.land(3)
    forward(ring(exp - 3, 8))
    forward(ring(exp + 3, 8))
    reduce_pass(1)
    rows.land(4)
    forward(ring(exp + 4, 8))

    dg[...] = jnp.zeros_like(dg)
    for index in range(count // BLOCK):
        at = pl.ds(index * BLOCK, BLOCK)
        act, slope = silu_parts(acc_a[at])
        up, back = acc_b[at], acc_u[at]
        hidden = act * up
        dg[:, at] = lax.dot_general(
            jnp.ones((16, hidden.shape[1]), F32),
            hidden * back,
            (((1,), (1,)), ((), ())),
            preferred_element_type=F32,
            precision=lax.Precision.HIGHEST,
        ).astype(BF16)
        scaled = gate[at] * back
        grad_a = (scaled * up * slope).astype(BF16)
        grad_b = (scaled * act).astype(BF16)
        hidden_w = (gate[at] * hidden).astype(BF16)
        da[at], db[at], hw[at] = grad_a, grad_b, hidden_w
        dat[:, at], dbt[:, at], hwt[:, at] = grad_a.T, grad_b.T, hidden_w.T

    def partial(piece):
        cols = pl.ds(pl.multiple_of(piece * width, 128), width)

        def block(index, carry):
            at = pl.ds(pl.multiple_of(index * BLOCK, BLOCK), BLOCK)
            pb[piece, at] = (dot(da[at], wg[:, cols]) + dot(db[at], wu[:, cols])).astype(BF16)
            return carry

        lax.fori_loop(0, count // BLOCK, block, 0)
        pb[piece, count : count + 16] = dg[...]
        pb[piece, count + 16 :] = dot_last(s_dab[...], ws[piece, :, : 2 * lanes]).astype(BF16)

    parts = (pl.ds(0, split), pl.ds(split, total - split))
    landed = (rp, rm)

    def sum_copy(step, way, sub):
        sign = 1 - 2 * way
        return remote(
            pb.at[ring(exp + sign * (5 - step), 8), parts[sub]],
            landed[way].at[step - 1, parts[sub]],
            p_s.at[way, sub, step - 1],
            p_r.at[way, sub, step - 1],
            (seq, ring(exp + sign, 8)),
        )

    def has_sum(step, way, sub):
        return step > 1 or way == sub

    def sum_step(step):
        for sub in range(2):
            for way in range(2):
                if has_sum(step - 1, way, sub):
                    sum_copy(step - 1, way, sub).wait_recv()
                    piece = ring(exp + (1 - 2 * way) * (5 - step), 8)
                    pb[piece, parts[sub]] = (
                        pb[piece, parts[sub]].astype(F32)
                        + landed[way][step - 2, parts[sub]].astype(F32)
                    ).astype(BF16)
                sum_copy(step, way, sub).start()

    outs = (out_gate, out_up, out_down)

    def out_copy(index, which):
        piece = ring(exp + index, 8)
        cols = pl.ds(pl.multiple_of(piece * width, 128), width)
        return pltpu.make_async_copy(
            stage.at[index % 2, which], outs[which].at[:, cols], o_s.at[index % 2, which]
        )

    def weight_grads(index):
        piece = ring(exp + index, 8)
        if index >= 2:
            for which in range(3):
                out_copy(index - 2, which).wait()
        stage[index % 2, 0] = dot(dat[...], xb[piece]).astype(BF16)
        stage[index % 2, 1] = dot(dbt[...], xb[piece]).astype(BF16)
        stage[index % 2, 2] = dot(hwt[...], yb[piece]).astype(BF16)
        for which in range(3):
            out_copy(index, which).start()

    partial(ring(exp + 4, 8))
    sum_copy(1, 0, 0).start()
    sum_copy(1, 1, 1).start()
    partial(ring(exp + 3, 8))
    partial(ring(exp - 3, 8))
    sum_step(2)
    partial(ring(exp + 2, 8))
    partial(ring(exp - 2, 8))
    reduce_end(1)
    out_shared[...] = gp[plane.x, plane.y, core]
    weight_grads(0)
    weight_grads(1)
    sum_step(3)
    partial(ring(exp + 1, 8))
    partial(ring(exp - 1, 8))
    weight_grads(2)
    weight_grads(3)
    sum_step(4)
    partial(exp)
    for index in range(4, 8):
        weight_grads(index)
    for sub in range(2):
        for way in range(2):
            sum_copy(4, way, sub).wait_recv()
    whole = pb[exp].astype(F32) + rp[3].astype(F32) + rm[3].astype(F32)
    row_sum[...] = whole[: count + 16].astype(BF16)
    shared_rows[...] = whole[count + 16 :]

    rows.finish()
    across.wait_send()
    for half in range(2):
        for phase in range(2):
            for kind in range(3):
                reduce_copy(half, phase, kind).wait_send()
    for step in range(1, 5):
        for way in range(2):
            for sub in range(2):
                if has_sum(step, way, sub):
                    sum_copy(step, way, sub).wait_send()
    for index in (6, 7):
        for which in range(3):
            out_copy(index, which).wait()


def expert(row_x, row_y, gate, w_gate, w_up, w_down, tok, grad, shared, collective_id):
    count, width = row_x.shape
    hidden, model = w_gate.shape
    tok_rows = tok.shape[1]
    total = count + 16 + tok_rows
    chunk, lanes = shared.shape[3:]
    dma = pltpu.SemaphoreType.DMA
    vmem = pltpu.VMEM
    routed = jax.ShapeDtypeStruct((hidden, model), BF16)
    return pl.pallas_call(
        expert_kernel,
        out_shape=(
            jax.ShapeDtypeStruct((count + 16, width), BF16),
            jax.ShapeDtypeStruct((tok_rows, width), F32),
            routed,
            routed,
            routed,
            jax.ShapeDtypeStruct((chunk, lanes), BF16),
        ),
        in_specs=any_specs(2) + vmem_specs(1) + any_specs(6),
        out_specs=vmem_specs(2) + any_specs(3) + vmem_specs(1),
        scratch_shapes=[
            vmem((8, count, width), BF16),
            vmem((8, count, width), BF16),
            vmem((hidden, model), BF16),
            vmem((hidden, model), BF16),
            vmem((hidden, model), BF16),
            vmem((8, tok_rows, width), BF16),
            vmem((8, tok_rows, width), BF16),
            vmem((8, width, lanes), BF16),
            vmem((tok_rows, lanes), F32),
            vmem((tok_rows, lanes // 3 * 2), BF16),
            vmem((tok_rows, lanes // 3), BF16),
            vmem((SIDE, SIDE, 2, chunk, lanes), BF16),
            vmem((SIDE, SIDE, chunk, lanes), BF16),
            vmem((2, 3, SIDE, chunk // 2, lanes), BF16),
            vmem((2, 3, chunk // 2, lanes), BF16),
            vmem((count, hidden), F32),
            vmem((count, hidden), F32),
            vmem((count, hidden), F32),
            vmem((count, hidden), BF16),
            vmem((count, hidden), BF16),
            vmem((count, hidden), BF16),
            vmem((hidden, count), BF16),
            vmem((hidden, count), BF16),
            vmem((hidden, count), BF16),
            vmem((16, width), BF16),
            vmem((8, total, width), BF16),
            vmem((4, total, width), BF16),
            vmem((4, total, width), BF16),
            vmem((2, 3, hidden, width), BF16),
            dma((8,)),
            dma((2, 2, 4)),
            dma((2, 2, 4)),
            dma,
            dma,
            dma((2, 2, 3)),
            dma((2, 2, 3)),
            dma((2, 2, 4)),
            dma((2, 2, 4)),
            dma((2, 3)),
        ],
        compiler_params=pltpu.CompilerParams(
            collective_id=collective_id, has_side_effects=True, vmem_limit_bytes=62 * MIB
        ),
    )(row_x, row_y, gate, w_gate, w_up, w_down, tok, grad, shared.reshape(8, width, lanes))


def with_side(rows, side, at):
    wide = jnp.pad(side, ((0, 0), (0, rows.shape[2] - side.shape[1])))
    row = lax.broadcasted_iota(jnp.int32, rows.shape, 1)
    return jnp.where(row == at, wide[:, None, :].astype(rows.dtype), rows)


def body(
    tokens, out_grad, expert_ids, gates, w_gate, w_up, w_down, shared_gate, shared_up, shared_down
):
    tok_rows, width = tokens.shape
    experts = 32
    window = jnp.arange(experts, dtype=jnp.int32)
    onehot = (expert_ids[:, :, None] == window).astype(F32)
    named = jnp.sum(onehot, axis=1)
    gate_of = jnp.sum(onehot * gates.astype(F32)[:, :, None], axis=1)
    order = jnp.arange(tok_rows, dtype=jnp.int32)
    earlier = (order[None, :] < order[:, None]).astype(BF16)
    rank = dot(earlier, named.astype(BF16))
    rank = jnp.where(named > 0, rank, -1.0)
    slots = jnp.arange(SLOT, dtype=jnp.int32).astype(F32)
    pick = (rank.T[:, None, :] == slots[None, :, None]).astype(F32)
    pick_flat = pick.astype(BF16).reshape(experts * SLOT, tok_rows)
    slot_gate = jnp.sum(pick * gate_of.T[:, None, :], axis=2)
    counts = jnp.broadcast_to(jnp.sum(named, axis=0)[None, :], (experts, experts))
    both = jnp.concatenate([tokens, out_grad], axis=1)
    send = dot(pick_flat, both).astype(BF16).reshape(experts, SLOT, 2 * width)
    send = with_side(with_side(send, slot_gate, MOST), counts, MOST + 1)

    def widen(part):
        return jnp.pad(part, ((0, 0), (0, 256 - part.shape[1])))

    shared = jnp.concatenate([widen(shared_gate), widen(shared_up), widen(shared_down.T)], axis=1)
    got, full_x, full_y, whole = spread(send, tokens, out_grad, shared)

    counts = got[:, MOST + 1, :experts].astype(F32)
    per_expert = jnp.sum(counts, axis=0)
    here = lax.axis_index("seq")
    mine = jnp.sum(jnp.where(window[None, :] == here, counts, 0.0), axis=1)
    first = jnp.sum(jnp.where(window[None, :] < window[:, None], mine[None, :], 0.0), axis=1)
    spot = jnp.where(slots[None, :] < mine[:, None], first[:, None] + slots[None, :], -1.0)
    got_gate = got[:, MOST, :SLOT].reshape(1, experts * SLOT).astype(F32)
    got_flat = got.reshape(experts * SLOT, 2 * width)

    def run(count, collective_id):
        index = jnp.arange(count, dtype=jnp.int32).astype(F32)
        pack = (spot.reshape(1, experts * SLOT) == index[:, None]).astype(F32)
        row_gate = jnp.sum(pack * got_gate, axis=1, keepdims=True)
        pack = pack.astype(BF16)
        row_x = dot(pack, got_flat[:, :width]).astype(BF16)
        row_y = dot(pack, got_flat[:, width:]).astype(BF16)
        row_sum, shared_rows, grad_gate, grad_up, grad_down, grad_shared = expert(
            row_x, row_y, row_gate, w_gate[0], w_up[0], w_down[0], full_x, full_y, whole, collective_id
        )
        rows = dot_rows(pack, row_sum[:count]).astype(BF16).reshape(experts, SLOT, width)
        route = jnp.sum(pack.astype(F32) * row_sum[count, :count].astype(F32)[:, None], axis=0)
        rows = with_side(rows, route.reshape(experts, SLOT), MOST)
        return rows, shared_rows, grad_gate, grad_up, grad_down, grad_shared

    rows, shared_rows, grad_gate, grad_up, grad_down, grad_shared = run(experts * MOST, 2)
    back = send_back(rows)
    routed = dot_rows(pick_flat, back.reshape(experts * SLOT, width))
    token_grad = (routed + shared_rows).astype(BF16)
    route = jnp.sum(pick * back[:, MOST, :SLOT].astype(F32)[:, :, None], axis=1)
    gate_grad = jnp.sum(onehot * route.T[:, None, :], axis=2)
    hidden = shared_gate.shape[1]
    return (
        token_grad,
        gate_grad,
        grad_gate[None],
        grad_up[None],
        grad_down[None],
        grad_shared[:, :hidden],
        grad_shared[:, 256 : 256 + hidden],
        grad_shared[:, 512 : 512 + hidden].T,
    )


def solution(mesh):
    return jax.shard_map(
        body,
        mesh=mesh,
        in_specs=(
            P("seq", "exp"),
            P("seq", "exp"),
            P("seq", None),
            P("seq", None),
            P("seq", "exp", None),
            P("seq", "exp", None),
            P("seq", "exp", None),
            P("seq", "exp"),
            P("seq", "exp"),
            P("exp", "seq"),
        ),
        out_specs=(
            P("seq", "exp"),
            P("seq", None),
            P("seq", "exp", None),
            P("seq", "exp", None),
            P("seq", "exp", None),
            P("seq", "exp"),
            P("seq", "exp"),
            P("exp", "seq"),
        ),
        check_vma=False,
    )
```

time: 727 us -> 250 us (0.34)
  waiting for transfers between devices: 522 us -> 0 us
  Pallas kernels: 0 us -> 221 us
  blocking collectives: 61.9 us -> 0 us
  local copies, waits for them, and re-layouts: 51.8 us -> 7.88 us
  matrix products: 44 us -> 9.1 us
  starting transfers between devices: 23.1 us -> 0 us
  between operations: 14.6 us -> 0.81 us
    all_gather x7 -> x0, waiting for transfers between devices: 246 us -> none  [the longest x1 55.3 us: body(): lax.all_gather(shared_down, 'seq', axis=1, tiled=True)]
    pallas_call x0 -> x3, Pallas kernels: none -> 221 us  [the longest x1 134 us: expert(): pl.pallas_call(expert_kernel, out_shape=(jax.ShapeDtypeStruct((count + 16...]
    unnamed x16 -> x0, waiting for transfers between devices: 220 us -> none
    reduce_scatter x1 -> x0, waiting for transfers between devices: 55.2 us -> none  [body(): lax.psum_scatter(part_d.astype(jnp.bfloat16), 'seq', scatter_dimension=1,...]
    all_to_all x3 -> x0, blocking collectives: 49.8 us -> none  [the longest x1 21.3 us: body(): lax.all_to_all(send_x, 'seq', split_axis=0, concat_axis=0, tiled=True)]
    all_to_all x2 -> x0, starting transfers between devices: 22.6 us -> none  [the longest x1 15.1 us: body(): lax.all_to_all(dgate_sum.astype(jnp.bfloat16), 'seq', split_axis=0, conca...]
    dot_general x10 -> x4, matrix products: 27.6 us -> 5.28 us  [dot(): return jnp.dot(left, right, preferred_element_type=F32)]
    gather x7 -> x0, local copies, waits for them, and re-layouts: 19.6 us -> none  [the longest x1 5.01 us: body(): gate_grad = padded_gate[slot].reshape(tok_rows, TOPK)]
  transfers between devices with their start and end apart: 14 -> 0, of which waited for: 11 -> 0; matrix products, arithmetic and copies ran while one was open for 13% -> 0% of each run, Pallas kernels for 0% -> 0%
where the time goes in v1:
time: 250 us
  Pallas kernels  221 us (88%)
  other arithmetic  10.7 us (4%)
  matrix products  9.1 us (4%)
  local copies, waits for them, and re-layouts  7.88 us (3%)
    pallas_call x1, Pallas kernels, expert(): pl.pallas_call(expert_kernel, out_shape=(jax.ShapeDtypeStruct((count + 16...  134 us
    pallas_call x1, Pallas kernels, spread(): pl.pallas_call(spread_kernel, out_shape=(jax.ShapeDtypeStruct(send.shape,...  67.4 us
    pallas_call x1, Pallas kernels, send_back(): pl.pallas_call(back_kernel, out_shape=jax.ShapeDtypeStruct(send.shape, BF...  19.9 us
    unnamed x17, local copies, waits for them, and re-layouts  5.8 us
    dot_general x4, matrix products, dot(): return jnp.dot(left, right, preferred_element_type=F32)  5.28 us

profile of v1, /device:TPU:1, one launch (start us, length us, event | category | flops | bytes accessed | tf_op | source)
XLA Modules:
  0.0 249.6 jit_solution(9939839767546604)
XLA Ops:
  0.7 0.7 convert_element_type.130
  1.4 0.1 lt.59
  1.5 0.8 convert_reduce_fusion
  2.3 0.1 convolution_select_fusion
  2.4 0.2 fusion.27
  2.7 0.1 convert_convert_fusion
  2.8 1.7 fusion.30.shared
  4.5 1.5 convolution_convert_fusion
  6.0 1.3 select_select_fusion.send
  7.3 67.4 %shard_map.161 = (bf16[32,16,1280]{2,1,0:T(8,128)(2,1)}, bf16[8,128,640]{2,1,0:T(8,128)(2,1)}, bf16[8,128,640]{2,1,0:T(8,128)(2,1)}, bf16[4,4,2,160,768]{4,3,2,1,0:T(8,128)(2,1)}) custom-call(bf16[32,16,1280]{2,1,0:T(8,128)(2,1)} %select_select_fusion.send, bf16[128,640]{1,0:T(8,128)(2,1)} %tok.1, bf16[128,640]{1,0:T(8,128)(2,1)} %grad.1, ...), custom_call_target="tpu_custom_call" | custom-call | tf_op jit(solution)/shard_map/pallas_call | solution.py:260
  74.7 0.0 copy-start.6
  74.7 1.0 convert_reduce_fusion.2
  75.8 0.1 reshape.130
  75.8 0.9 slice_convert_fusion.1
  76.7 0.1 select_reduce_fusion.3
  76.8 0.1 select_reduce_fusion.2
  76.9 0.1 lt.60
  77.0 0.1 lt.61
  77.1 0.1 add.32
  77.1 0.1 add.33
  77.2 0.2 fusion.9
  77.5 0.8 broadcast_in_dim.102.gate
  78.3 2.4 convolution_convert_fusion.2.row_y
  80.7 0.0 copy-done.6
  80.7 1.3 convolution_convert_fusion.3.row_x
  82.0 133.8 %shard_map.162 = (bf16[400,640]{1,0:T(8,128)(2,1)}, f32[128,640]{1,0:T(8,128)}, bf16[192,5120]{1,0:T(8,128)(2,1)}, bf16[192,5120]{1,0:T(8,128)(2,1)}, bf16[192,5...) custom-call(bf16[384,640]{1,0:T(8,128)(2,1)} %convolution_convert_fusion.3.row_x, ...), custom_call_target="tpu_custom_call" | custom-call | tf_op jit(solution)/shard_map/pallas_call | solution.py:630
  215.8 0.7 convert_reduce_fusion.3
  216.5 0.2 fusion.8
  216.7 0.1 reshape.127
  216.8 1.7 convolution_convert_fusion.1
  218.5 0.0 copy-start.3
  218.5 1.0 broadcast_select_fusion.send
  219.5 0.0 copy-start.5
  219.5 19.9 %shard_map.163 = bf16[32,16,640]{2,1,0:T(8,128)(2,1)} custom-call(bf16[32,16,640]{2,1,0:T(8,128)(2,1)} %broadcast_select_fusion.send), custom_call_target="tpu_custom_call" | custom-call | tf_op jit(solution)/shard_map/pallas_call | solution.py:324
  239.4 0.0 copy-done.3
  239.4 2.1 fusion.1
  241.5 0.9 slice_convert_fusion
  242.4 0.1 fusion.28
  242.5 0.0 copy-done.5
  242.6 0.6 select_reduce_fusion
  243.2 0.0 copy-done.4
  243.2 0.7 slice_bitcast_fusion
  243.9 0.0 copy-done.2
  243.9 1.3 copy.35
  245.1 1.0 copy-done.1
  246.1 1.3 copy.36
  247.4 1.0 copy-done
  248.4 1.3 copy.37
  (13 shorter events, 0.1 us)
Async XLA Ops:
  74.7 5.9 %copy-start.6 = (bf16[32,16,1280]{2,1,0:T(8,128)(2,1)S(1)}, bf16[32,16,1280]{2,1,0:T(8,128)(2,1)}, u32[]{:S(2)}) copy-start(bf16[32,16,1280]{2,1,0:T(8,128)(2,1)} %get-tuple-element.18) | copy-start | bytes 3932164
  218.5 20.9 %copy-start.3 = (f32[128,640]{1,0:T(8,128)S(1)}, f32[128,640]{1,0:T(8,128)}, u32[]{:S(2)}) copy-start(f32[128,640]{1,0:T(8,128)} %get-tuple-element.23) | copy-start | bytes 983044
  219.5 23.1 %copy-start.5 = (s32[128,6]{0,1:T(8,128)S(1)}, s32[128,6]{0,1:T(8,128)}, u32[]{:S(2)}) copy-start(s32[128,6]{0,1:T(8,128)} %param.12) | copy-start | bytes 9220
  219.5 23.7 %copy-start.4 = (bf16[160,768]{1,0:T(8,128)(2,1)S(1)}, bf16[160,768]{1,0:T(8,128)(2,1)}, u32[]{:S(2)}) copy-start(bf16[160,768]{1,0:T(8,128)(2,1)} %get-tuple-element.27) | copy-start | bytes 737284
  219.5 24.4 %copy-start.2 = (bf16[192,5120]{1,0:T(8,128)(2,1)S(1)}, bf16[192,5120]{1,0:T(8,128)(2,1)}, u32[]{:S(2)}) copy-start(bf16[192,5120]{1,0:T(8,128)(2,1)} %get-tuple-element.24) | copy-start | bytes 5898244
  243.9 2.3 copy-start.1
  246.1 2.3 copy-start

commit v2 on v1

v2 whole, which is shorter than its diff:
```python
import functools

import jax
import jax.numpy as jnp
from jax import lax
from jax.experimental import pallas as pl
from jax.experimental.pallas import tpu as pltpu
from jax.sharding import PartitionSpec as P

MESH = pl.DeviceIdType.MESH
MOST = 12
SLOT = 16
SIDE = 4
BLOCK = 128
FAR = 1
MIB = 1 << 20
F32 = jnp.float32
BF16 = jnp.bfloat16


def dot(left, right):
    return jnp.dot(left, right, preferred_element_type=F32)


def dot_last(left, right):
    return lax.dot_general(left, right, (((1,), (1,)), ((), ())), preferred_element_type=F32)


def dot_rows(left, right):
    return lax.dot_general(left, right, (((0,), (0,)), ((), ())), preferred_element_type=F32)


def silu_parts(value):
    sig = jax.nn.sigmoid(value)
    return value * sig, sig * (1.0 + value * (1.0 - sig))


def ring(value, size):
    return lax.rem(value + size, size)


def place():
    seq, exp = lax.axis_index("seq"), lax.axis_index("exp")
    return (
        seq,
        exp,
        lax.div(seq, 2 * SIDE),
        lax.rem(lax.div(seq, 2), SIDE),
        lax.rem(seq, 2),
    )


def remote(src, dst, send_sem, recv_sem, device):
    return pltpu.make_async_remote_copy(
        src_ref=src,
        dst_ref=dst,
        send_sem=send_sem,
        recv_sem=recv_sem,
        device_id=device,
        device_id_type=MESH,
    )


def greet(barrier, device):
    pl.semaphore_signal(barrier, inc=1, device_id=device, device_id_type=MESH)


class ZRing:
    def __init__(self, own, bufs, seq, exp, send_sem, recv_sem, full=3, half=True):
        self.own, self.bufs, self.seq, self.exp = own, bufs, seq, exp
        self.send_sem, self.recv_sem = send_sem, recv_sem
        self.full, self.half = full, half

    def has(self, step, way, sub):
        return step <= self.full or (self.half and step == self.full + 1 and way == sub)

    def copy(self, step, way, sub, landed=False):
        sign = 1 - 2 * way
        piece = ring(self.exp - sign * (step if landed else step - 1), 8)
        slot = self.bufs[sub].at[piece]
        src = self.own[sub] if step == 1 and not landed else slot
        return remote(
            src,
            slot,
            self.send_sem.at[way, sub, step - 1],
            self.recv_sem.at[way, sub, step - 1],
            (self.seq, ring(self.exp + sign, 8)),
        )

    def start(self, step):
        for sub in range(2):
            for way in range(2):
                if self.has(step, way, sub):
                    self.copy(step, way, sub).start()

    def land(self, step):
        for sub in range(2):
            for way in range(2):
                if self.has(step, way, sub):
                    self.copy(step, way, sub, landed=True).wait_recv()
                    if self.has(step + 1, way, sub):
                        self.copy(step + 1, way, sub).start()

    def finish(self):
        for step in range(1, 5):
            for sub in range(2):
                for way in range(2):
                    if self.has(step, way, sub):
                        self.copy(step, way, sub).wait_send()


class ZSum:
    def __init__(self, own, landed, split, seq, exp, send_sem, recv_sem):
        self.own, self.landed, self.seq, self.exp = own, landed, seq, exp
        self.send_sem, self.recv_sem = send_sem, recv_sem
        self.parts = (pl.ds(0, split), pl.ds(split, own.shape[1] - split))

    def has(self, step, way, sub):
        return step > 1 or way == sub

    def copy(self, step, way, sub):
        sign = 1 - 2 * way
        return remote(
            self.own.at[ring(self.exp + sign * (5 - step), 8), self.parts[sub]],
            self.landed[way].at[step - 1, self.parts[sub]],
            self.send_sem.at[way, sub, step - 1],
            self.recv_sem.at[way, sub, step - 1],
            (self.seq, ring(self.exp + sign, 8)),
        )

    def step(self, step):
        for sub in range(2):
            for way in range(2):
                if step > 1 and self.has(step - 1, way, sub):
                    self.copy(step - 1, way, sub).wait_recv()
                    piece = ring(self.exp + (1 - 2 * way) * (5 - step), 8)
                    part = self.parts[sub]
                    self.own[piece, part] = (
                        self.own[piece, part].astype(F32) + self.landed[way][step - 2, part].astype(F32)
                    ).astype(BF16)
                if self.has(step, way, sub):
                    self.copy(step, way, sub).start()

    def total(self):
        for sub in range(2):
            for way in range(2):
                self.copy(4, way, sub).wait_recv()
        return sum(part.astype(F32) for part in (self.own[self.exp], self.landed[0][3], self.landed[1][3]))

    def finish(self):
        for step in range(1, 5):
            for way in range(2):
                for sub in range(2):
                    if self.has(step, way, sub):
                        self.copy(step, way, sub).wait_send()


class Plane:
    def __init__(self):
        self.seq, self.exp, self.x, self.y, self.core = place()

    def device(self, along_x, step):
        x = ring(self.x + step, SIDE) if along_x else self.x
        y = self.y if along_x else ring(self.y + step, SIDE)
        return ((x * SIDE + y) * 2 + self.core, self.exp)

    def view(self, ref, half, wide, along_x, step):
        count = ref.shape[3] // 2
        rows = pl.ds(half * count, count)
        here = ring((self.x if along_x else self.y) + step, SIDE)
        if along_x:
            return ref.at[here, :, self.core, rows] if wide else ref.at[here, self.y, self.core, rows]
        return ref.at[:, here, self.core, rows] if wide else ref.at[self.x, here, self.core, rows]


def one_hot(rows, columns, shift):
    row = lax.broadcasted_iota(jnp.int32, (rows, columns), 0)
    column = lax.broadcasted_iota(jnp.int32, (rows, columns), 1)
    return jnp.where(row == column + shift, 1.0, 0.0).astype(BF16)


def half_lanes(rows, high):
    lane = lax.broadcasted_iota(jnp.int32, (rows, 128), 1)
    return jnp.where((lane >= 64) == high, 1.0, 0.0).astype(BF16)


def layer_kernel(
    ids, gates, tok, grad, w_gate, w_up, w_down, shared_gate, shared_up, shared_down,
    out_tok, out_route, out_gate, out_up, out_down, out_shared,
    pick, send, got, far_send, far_got, pack, gate, xb, yb, wg, wu, wd, tx, ty, ws,
    s_acc, s_dab, s_h, gp, sib, qa, qb,
    acc_a, acc_b, acc_u, da, db, hw, dat, dbt, hwt, dg,
    pb, rp, rm, sb, sp, sm, stage, send_b, got_b,
    own_sem, a_s, a_r, f_s, f_r, t_s, t_r, w_s, w_r, b_s, b_r, z_s, z_r, c_s, c_r, q_s, q_r,
    p_s, p_r, g_s, g_r, o_s, e_s, e_r,
):
    plane = Plane()
    seq, exp, core = plane.seq, plane.exp, plane.core
    sibling = (seq + 1 - 2 * core, exp)
    count = pack.shape[0]
    tok_rows, width = tok.shape
    slots = send.shape[0]
    of_x, lanes = s_dab.shape[1], ws.shape[4]

    own = [
        pltpu.make_async_copy(src, dst, own_sem.at[i])
        for i, (src, dst) in enumerate(
            ((tok, tx.at[exp]), (grad, ty.at[exp]), (w_gate, wg), (w_up, wu), (w_down, wd))
        )
    ]
    for copy in own:
        copy.start()

    barrier = pltpu.get_barrier_semaphore()

    def hello(step, carry):
        greet(barrier, (ring(seq + step, 32), exp))
        return carry

    lax.fori_loop(1, 32, hello, 0)
    greet(barrier, (seq, ring(exp + 1, 8)))
    greet(barrier, (seq, ring(exp - 1, 8)))

    experts = slots // SLOT
    expert = lax.broadcasted_iota(jnp.int32, (experts, tok_rows), 0)
    named = jnp.zeros((experts, tok_rows), F32)
    gate_of = jnp.zeros((experts, tok_rows), F32)
    for k in range(ids.shape[0]):
        hit = ids[k : k + 1] == expert
        named += jnp.where(hit, 1.0, 0.0)
        gate_of += jnp.where(hit, gates[k : k + 1].astype(F32), 0.0)
    row = lax.broadcasted_iota(jnp.int32, (tok_rows, tok_rows), 0)
    lane = lax.broadcasted_iota(jnp.int32, (tok_rows, tok_rows), 1)
    earlier = jnp.where(row < lane, 1.0, 0.0)
    rank = jnp.where(named > 0.0, dot(named.astype(BF16), earlier.astype(BF16)), -1.0)
    slot = lax.broadcasted_iota(jnp.int32, (slots, experts), 0)
    to_expert = lax.shift_right_logical(slot, 4) == lax.broadcasted_iota(jnp.int32, (slots, experts), 1)
    spread = jnp.where(to_expert, 1.0, 0.0).astype(BF16)
    slot = lax.broadcasted_iota(jnp.int32, (slots, tok_rows), 0)
    picked = dot(spread, rank.astype(BF16)) == lax.bitwise_and(slot, SLOT - 1).astype(F32)
    pick[...] = jnp.where(picked, 1.0, 0.0).astype(BF16)

    units = shared_gate.shape[1]
    ws[plane.x, plane.y, core, :, :128] = shared_gate[:, :128]
    ws[plane.x, plane.y, core, :, 128:256] = shared_up[:, :128]
    ws[plane.x, plane.y, core, :, 256:384] = (
        dot(shared_gate[...], one_hot(units, 128, 128)) + dot(shared_up[...], one_hot(units, 128, 64) * half_lanes(units, True))
    ).astype(BF16)
    ws[plane.x, plane.y, core, :, 384:512] = shared_down[:, :128]
    ws[plane.x, plane.y, core, :, 512:] = dot(shared_down[...], one_hot(units, 128, 128)).astype(BF16)
    pl.semaphore_wait(barrier, 33)

    tokens = ZRing((tok, grad), (tx, ty), seq, exp, t_s, t_r)
    tokens.start(1)

    def exchange(src, dst, s_sem, r_sem, step, landed):
        to, source = ring(seq + step, 32), ring(seq - step, 32)
        at = (source if landed else seq) * SLOT
        return remote(
            src.at[pl.ds(pl.multiple_of(to * SLOT, SLOT), SLOT)],
            dst.at[pl.ds(pl.multiple_of(at, SLOT), SLOT)],
            s_sem.at[step - 1],
            r_sem.at[step - 1],
            (to, exp),
        )

    def exchange_start(src, dst, s_sem, r_sem, first=1, last=31):
        def one(step, carry):
            exchange(src, dst, s_sem, r_sem, step, False).start()
            return carry

        lax.fori_loop(first, last + 1, one, 0)
        if first == 1:
            here = pl.ds(pl.multiple_of(seq * SLOT, SLOT), SLOT)
            dst[here] = src[here]

    def exchange_end(src, dst, s_sem, r_sem):
        def one(step, carry):
            exchange(src, dst, s_sem, r_sem, step, True).wait_recv()
            return carry

        lax.fori_loop(1, 32, one, 0)

    def exchange_sent(src, dst, s_sem, r_sem):
        def one(step, carry):
            exchange(src, dst, s_sem, r_sem, step, False).wait_send()
            return carry

        lax.fori_loop(1, 32, one, 0)

    out_going = (send, got, a_s, a_r)
    far_going = (far_send, far_got, f_s, f_r)
    home_going = (send_b, got_b, e_s, e_r)

    def weight(half, phase, kind, landed):
        along_x = half != phase
        sign = 1 - 2 * half
        wide = phase == 1
        if kind == 0:
            to, piece = sign, (-sign if landed else 0)
        elif kind == 1:
            to, piece = -sign, (sign if landed else 0)
        else:
            to, piece = sign, (2 if landed else -sign)
        part = plane.view(ws, half, wide, along_x, piece)
        return remote(
            part, part, w_s.at[half, phase, kind], w_r.at[half, phase, kind], plane.device(along_x, to)
        )

    def handed(half, phase, index, landed):
        along_x = half != phase
        sign = 1 - 2 * half
        wide = phase == 1
        piece = (0, -sign, sign, 2)[index]
        if landed:
            plane.core = 1 - core
        part = plane.view(ws, half, wide, along_x, piece)
        plane.core = core
        return remote(part, part, b_s.at[half, phase, index], b_r.at[half, phase, index], sibling)

    def weight_near(phase):
        for half in range(2):
            weight(half, phase, 0, True).wait_recv()
            weight(half, phase, 2, False).start()
            handed(half, phase, 1, False).start()
            weight(half, phase, 1, True).wait_recv()
            handed(half, phase, 2, False).start()

    def weight_far(phase):
        for half in range(2):
            weight(half, phase, 2, True).wait_recv()
            if phase == 0:
                weight(half, 1, 0, False).start()
                weight(half, 1, 1, False).start()
            handed(half, phase, 3, False).start()

    for half in range(2):
        weight(half, 0, 0, False).start()
        weight(half, 0, 1, False).start()
        handed(half, 0, 0, False).start()

    send[:, :width] = dot(pick[...], tok[...]).astype(BF16)
    send[:, width : 2 * width] = dot(pick[...], grad[...]).astype(BF16)
    slot_gate = jnp.where(picked, dot(spread, gate_of.astype(BF16)), 0.0)
    slot_gate = jnp.sum(slot_gate, axis=1, keepdims=True)
    send[:, 2 * width :] = jnp.broadcast_to(slot_gate, (slots, 128)).astype(BF16)

    exchange_start(*out_going)

    packed = lax.broadcasted_iota(jnp.int32, pack.shape, 0)
    source = lax.broadcasted_iota(jnp.int32, pack.shape, 1)
    rank = lax.bitwise_and(source, SLOT - 1)
    same = packed == lax.shift_right_logical(source, 4) * MOST + rank
    pack[...] = jnp.where(same & (rank < MOST), 1.0, 0.0).astype(BF16)
    acc_a[...] = jnp.zeros_like(acc_a)
    acc_b[...] = jnp.zeros_like(acc_b)
    acc_u[...] = jnp.zeros_like(acc_u)
    s_acc[...] = jnp.zeros_like(s_acc)
    dg[...] = jnp.zeros_like(dg)

    tokens.land(1)
    weight_near(0)
    tokens.land(2)
    exchange_end(*out_going)
    xb[exp] = dot(pack[...], got[:, :width]).astype(BF16)
    yb[exp] = dot(pack[...], got[:, width : 2 * width]).astype(BF16)
    rows = ZRing((xb.at[exp], yb.at[exp]), (xb, yb), seq, exp, z_s, z_r, 4 - FAR, FAR == 2)
    rows.start(1)
    weight_far(0)
    tokens.land(3)
    tokens.land(4)

    far = [(tx, xb, 4), (ty, yb, 4), (tx, xb, 3), (ty, yb, -3)][: 2 * FAR]
    for copy in own[:2]:
        copy.wait()
    for index, (tokens_of, _, step) in enumerate(far):
        at = slice(index * width, (index + 1) * width)
        far_send[:, at] = dot(pick[...], tokens_of[ring(exp + step, 8)]).astype(BF16)
    exchange_start(*far_going, 1, 8)
    gate[...] = dot(pack[...], got[:, 2 * width :])
    for copy in own[2:]:
        copy.wait()

    def forward(piece):
        cols = pl.ds(pl.multiple_of(piece * width, 128), width)

        acc_a[...] += dot_last(xb[piece], wg[:, cols])
        acc_b[...] += dot_last(xb[piece], wu[:, cols])
        acc_u[...] += dot_last(yb[piece], wd[:, cols])

    def weight_slice(piece, start, size):
        at_x, at_y = lax.div(piece, 2), 2 * lax.rem(piece, 2)
        return ws[at_x, pl.ds(at_y, 2), :, :, start : start + size].reshape(width, size)

    def shared_partial(piece, carry):
        sb[piece] = dot_last(s_dab[...], weight_slice(piece, 0, of_x)).astype(BF16)
        return carry


    def landing(half, phase, kind):
        return qb.at[half, kind] if phase else qa.at[half, kind]

    def reduce_copy(half, phase, kind):
        along_x = half == phase
        sign = 1 - 2 * half
        piece, to = ((2, sign), (-sign, -sign), (sign, sign))[kind]
        return remote(
            plane.view(gp, half, phase == 0, along_x, piece),
            landing(half, phase, kind),
            q_s.at[half, phase, kind],
            q_r.at[half, phase, kind],
            plane.device(along_x, to),
        )

    def reduce_add(half, phase, step, kinds):
        mine = plane.view(gp, half, phase == 0, half == phase, step)
        value = mine[...].astype(F32)
        for kind in kinds:
            value += landing(half, phase, kind)[...].astype(F32)
        mine[...] = value.astype(BF16)

    def reduce_start(phase):
        for half in range(2):
            reduce_copy(half, phase, 0).start()
            reduce_copy(half, phase, 1).start()

    def reduce_pass(phase):
        for half in range(2):
            reduce_copy(half, phase, 0).wait_recv()
            reduce_add(half, phase, 1 - 2 * half, (0,))
            reduce_copy(half, phase, 2).start()

    def reduce_end(phase):
        for half in range(2):
            reduce_copy(half, phase, 1).wait_recv()
            reduce_copy(half, phase, 2).wait_recv()
            reduce_add(half, phase, 0, (1, 2))

    forward(exp)
    weight_near(1)
    exchange_start(*far_going, 9, 16)
    rows.land(1)
    exchange_start(*far_going, 17, 24)
    forward(ring(exp - 1, 8))
    forward(ring(exp + 1, 8))
    weight_far(1)
    exchange_start(*far_going, 25, 31)
    for half in range(2):
        for phase in range(2):
            for index in range(phase, 4):
                handed(half, phase, index, True).wait_recv()

    def shared_forward(piece, carry):
        s_acc[:, :of_x] += dot(tx[piece], weight_slice(piece, 0, of_x))
        s_acc[:, of_x:] += dot(ty[piece], weight_slice(piece, of_x, lanes - of_x))
        return carry

    lax.fori_loop(0, 8, shared_forward, 0)
    act, slope = silu_parts(s_acc[:, :128])
    up, back = s_acc[:, 128:256], s_acc[:, 384:512]
    s_dab[:, :128] = (back * up * slope).astype(BF16)
    s_dab[:, 128:256] = (back * act).astype(BF16)
    s_h[:, :128] = (act * up).astype(BF16)
    act, slope = silu_parts(s_acc[:, 256:384])
    up, back = pltpu.roll(s_acc[:, 256:384], 64, 1), s_acc[:, 512:]
    s_dab[:, 256:] = (back * up * slope + pltpu.roll(back * act, 64, 1)).astype(BF16)
    s_h[:, 128:] = jnp.where(lane < 64, act * up, 0.0).astype(BF16)

    def shared_grads(piece, carry):
        at_x, at_y = lax.div(piece, 2), 2 * lax.rem(piece, 2)
        part = dot_rows(tx[piece], s_dab[...]).astype(BF16)
        gp[at_x, pl.ds(at_y, 2), :, :, :of_x] = part.reshape(2, 2, width // 4, of_x)
        part = dot_rows(ty[piece], s_h[...]).astype(BF16)
        gp[at_x, pl.ds(at_y, 2), :, :, of_x:] = part.reshape(2, 2, width // 4, lanes - of_x)
        return carry

    lax.fori_loop(0, 8, shared_grads, 0)
    across = remote(gp.at[:, :, 1 - core], sib, c_s, c_r, sibling)
    across.start()

    rows.land(2)
    forward(ring(exp - 2, 8))
    forward(ring(exp + 2, 8))
    across.wait_recv()

    def add_sibling(index, carry):
        at_x, at_y = lax.div(index, SIDE), lax.rem(index, SIDE)
        gp[at_x, at_y, core] = (
            gp[at_x, at_y, core].astype(F32) + sib[at_x, at_y].astype(F32)
        ).astype(BF16)
        return carry

    lax.fori_loop(0, SIDE * SIDE, add_sibling, 0)
    reduce_start(0)
    lax.fori_loop(0, 8, shared_partial, 0)
    shared_sums = ZSum(sb, (sp, sm), tok_rows // 2, seq, exp, g_s, g_r)
    shared_sums.step(1)
    exchange_end(*far_going)
    for index, (_, rows_of, step) in enumerate(far):
        at = slice(index * width, (index + 1) * width)
        rows_of[ring(exp + step, 8)] = dot(pack[...], far_got[:, at]).astype(BF16)
    forward(ring(exp + 4, 8))
    rows.land(3)
    shared_sums.step(2)
    forward(ring(exp - 3, 8))
    forward(ring(exp + 3, 8))

    for index in range(count // BLOCK):
        at = pl.ds(index * BLOCK, BLOCK)
        act, slope = silu_parts(acc_a[at])
        up, back = acc_b[at], acc_u[at]
        hidden = act * up
        dg[:, at] = lax.dot_general(
            jnp.ones((16, hidden.shape[1]), F32),
            hidden * back,
            (((1,), (1,)), ((), ())),
            preferred_element_type=F32,
            precision=lax.Precision.HIGHEST,
        ).astype(BF16)
        row_gate = gate[at, 0:1]
        scaled = row_gate * back
        grad_a = (scaled * up * slope).astype(BF16)
        grad_b = (scaled * act).astype(BF16)
        hidden_w = (row_gate * hidden).astype(BF16)
        da[at], db[at], hw[at] = grad_a, grad_b, hidden_w
        dat[:, at], dbt[:, at], hwt[:, at] = grad_a.T, grad_b.T, hidden_w.T

    def partial(piece):
        cols = pl.ds(pl.multiple_of(piece * width, 128), width)
        pb[piece, :count] = (dot(da[...], wg[:, cols]) + dot(db[...], wu[:, cols])).astype(BF16)
        pb[piece, count:] = dg[...]

    row_sums = ZSum(pb, (rp, rm), -(-pb.shape[1] // 32) * 16, seq, exp, p_s, p_r)

    outs = (out_gate, out_up, out_down)

    def out_copy(index, which):
        piece = ring(exp + index, 8)
        cols = pl.ds(pl.multiple_of(piece * width, 128), width)
        return pltpu.make_async_copy(
            stage.at[index % 2, which], outs[which].at[:, cols], o_s.at[index % 2, which]
        )

    def weight_grads(index):
        piece = ring(exp + index, 8)
        if index >= 2:
            for which in range(3):
                out_copy(index - 2, which).wait()
        stage[index % 2, 0] = dot(dat[...], xb[piece]).astype(BF16)
        stage[index % 2, 1] = dot(dbt[...], xb[piece]).astype(BF16)
        stage[index % 2, 2] = dot(hwt[...], yb[piece]).astype(BF16)
        for which in range(3):
            out_copy(index, which).start()

    partial(ring(exp + 4, 8))
    row_sums.step(1)
    partial(ring(exp + 3, 8))
    partial(ring(exp - 3, 8))
    row_sums.step(2)
    reduce_pass(0)
    partial(ring(exp + 2, 8))
    partial(ring(exp - 2, 8))
    weight_grads(0)
    row_sums.step(3)
    reduce_end(0)
    reduce_start(1)
    partial(ring(exp + 1, 8))
    partial(ring(exp - 1, 8))
    weight_grads(1)
    weight_grads(2)
    weight_grads(3)
    row_sums.step(4)
    shared_sums.step(3)
    reduce_pass(1)
    partial(exp)
    for index in range(4, 8):
        weight_grads(index)
    whole = row_sums.total()

    send_b[:, :width] = dot_rows(pack[...], whole[:count].astype(BF16)).astype(BF16)
    route = whole[count : count + 16, :count].T[:, 0:1]
    route = jnp.broadcast_to(route, (count, 128)).astype(BF16)
    send_b[:, width:] = dot_rows(pack[...], route).astype(BF16)
    exchange_start(*home_going)
    shared_sums.step(4)

    tokens.finish()
    rows.finish()
    row_sums.finish()
    reduce_end(1)
    out_shared[...] = gp[plane.x, plane.y, core]
    exchange_sent(*out_going)
    exchange_sent(*far_going)
    across.wait_send()
    for half in range(2):
        for phase in range(2):
            for kind in range(3):
                weight(half, phase, kind, False).wait_send()
                reduce_copy(half, phase, kind).wait_send()
            for index in range(phase, 4):
                handed(half, phase, index, False).wait_send()
    for index in (6, 7):
        for which in range(3):
            out_copy(index, which).wait()

    shared_rows = shared_sums.total()
    exchange_end(*home_going)
    out_tok[...] = (dot_rows(pick[...], got_b[:, :width]) + shared_rows).astype(BF16)
    routes = jnp.where(picked, got_b[:, width:].astype(F32), 0.0).astype(BF16)
    routes = dot_rows(spread, routes)
    for k in range(ids.shape[0]):
        hit = jnp.where(ids[k : k + 1] == expert, routes, 0.0)
        out_route[k : k + 1] = jnp.sum(hit, axis=0, keepdims=True)
    exchange_sent(*home_going)
    shared_sums.finish()


def any_specs(count):
    return [pl.BlockSpec(memory_space=pl.ANY)] * count


def vmem_specs(count):
    return [pl.BlockSpec(memory_space=pltpu.VMEM)] * count


def layer(ids, gates, tok, grad, w_gate, w_up, w_down, shared_gate, shared_up, shared_down):
    hidden, model = w_gate.shape
    tok_rows, width = tok.shape
    experts = model // shared_gate.shape[0]
    slots, count = experts * SLOT, experts * MOST
    chunk, lanes, of_x = shared_gate.shape[0], 640, 384
    dma = pltpu.SemaphoreType.DMA
    vmem = pltpu.VMEM
    routed = jax.ShapeDtypeStruct((hidden, model), BF16)
    return pl.pallas_call(
        layer_kernel,
        out_shape=(
            jax.ShapeDtypeStruct((tok_rows, width), BF16),
            jax.ShapeDtypeStruct(ids.shape, F32),
            routed,
            routed,
            routed,
            jax.ShapeDtypeStruct((chunk, lanes), BF16),
        ),
        in_specs=vmem_specs(4) + any_specs(3) + vmem_specs(3),
        out_specs=vmem_specs(2) + any_specs(3) + vmem_specs(1),
        scratch_shapes=[
            vmem((slots, tok_rows), BF16),
            vmem((slots, 2 * width + 128), BF16),
            vmem((slots, 2 * width + 128), BF16),
            vmem((slots, 2 * FAR * width), BF16),
            vmem((slots, 2 * FAR * width), BF16),
            vmem((count, slots), BF16),
            vmem((count, 128), F32),
            vmem((8, count, width), BF16),
            vmem((8, count, width), BF16),
            vmem((hidden, model), BF16),
            vmem((hidden, model), BF16),
            vmem((hidden, model), BF16),
            vmem((8, tok_rows, width), BF16),
            vmem((8, tok_rows, width), BF16),
            vmem((SIDE, SIDE, 2, chunk, lanes), BF16),
            vmem((tok_rows, lanes), F32),
            vmem((tok_rows, of_x), BF16),
            vmem((tok_rows, lanes - of_x), BF16),
            vmem((SIDE, SIDE, 2, chunk, lanes), BF16),
            vmem((SIDE, SIDE, chunk, lanes), BF16),
            vmem((2, 3, SIDE, chunk // 2, lanes), BF16),
            vmem((2, 3, chunk // 2, lanes), BF16),
            vmem((count, hidden), F32),
            vmem((count, hidden), F32),
            vmem((count, hidden), F32),
            vmem((count, hidden), BF16),
            vmem((count, hidden), BF16),
            vmem((count, hidden), BF16),
            vmem((hidden, count), BF16),
            vmem((hidden, count), BF16),
            vmem((hidden, count), BF16),
            vmem((16, width), BF16),
            vmem((8, count + 16, width), BF16),
            vmem((4, count + 16, width), BF16),
            vmem((4, count + 16, width), BF16),
            vmem((8, tok_rows, width), BF16),
            vmem((4, tok_rows, width), BF16),
            vmem((4, tok_rows, width), BF16),
            vmem((2, 3, hidden, width), BF16),
            vmem((slots, width + 128), BF16),
            vmem((slots, width + 128), BF16),
            dma((5,)),
            dma((31,)),
            dma((31,)),
            dma((31,)),
            dma((31,)),
            dma((2, 2, 4)),
            dma((2, 2, 4)),
            dma((2, 2, 3)),
            dma((2, 2, 3)),
            dma((2, 2, 4)),
            dma((2, 2, 4)),
            dma((2, 2, 4)),
            dma((2, 2, 4)),
            dma,
            dma,
            dma((2, 2, 3)),
            dma((2, 2, 3)),
            dma((2, 2, 4)),
            dma((2, 2, 4)),
            dma((2, 2, 4)),
            dma((2, 2, 4)),
            dma((2, 3)),
            dma((31,)),
            dma((31,)),
        ],
        compiler_params=pltpu.CompilerParams(
            collective_id=0, has_side_effects=True, vmem_limit_bytes=62 * MIB
        ),
    )(ids, gates, tok, grad, w_gate, w_up, w_down, shared_gate, shared_up, shared_down)


PARTS = 4


def finish_kernel(
    tok, route, shared, in_gate, in_up, in_down,
    out_tok, out_route, out_gate, out_up, out_down, shared_gate, shared_up, shared_down,
):
    out_gate[...] = in_gate[...]
    out_up[...] = in_up[...]
    out_down[...] = in_down[...]

    @pl.when(pl.program_id(0) == 0)
    def _():
        out_tok[...] = tok[...]
        out_route[...] = route[...]
        units = shared_gate.shape[1]
        shared_gate[:, :128] = shared[:, :128]
        shared_gate[:, 128:] = shared[:, 256 : 256 + units - 128]
        shared_up[:, :128] = shared[:, 128:256]
        shared_up[:, 128:] = dot(shared[:, 256:384], one_hot(128, units - 128, 64)).astype(BF16)
        shared_down[:, :128] = shared[:, 384:512]
        shared_down[:, 128:] = shared[:, 512 : 512 + units - 128]


def finish(tok, route, shared, grads, shared_shapes):
    shapes = [tok, route, *grads, *shared_shapes]
    hidden, model = grads[0].shape

    def whole(part):
        return pl.BlockSpec(part.shape, lambda step: (0, 0))

    band = [pl.BlockSpec((hidden // PARTS, model), lambda step: (step, 0))] * 3
    return pl.pallas_call(
        finish_kernel,
        grid=(PARTS,),
        out_shape=tuple(jax.ShapeDtypeStruct(part.shape, part.dtype) for part in shapes),
        in_specs=[whole(tok), whole(route), whole(shared), *band],
        out_specs=[whole(tok), whole(route), *band, *map(whole, shared_shapes)],
        compiler_params=pltpu.CompilerParams(vmem_limit_bytes=62 * MIB),
    )(tok, route, shared, *grads)


def body(
    tokens, out_grad, expert_ids, gates, w_gate, w_up, w_down, shared_gate, shared_up, shared_down
):
    shared = (shared_gate, shared_up, shared_down.T)
    token_grad, route, grad_gate, grad_up, grad_down, grad_shared = layer(
        expert_ids.T, gates.T, tokens, out_grad, w_gate[0], w_up[0], w_down[0], *shared
    )
    token_grad, route, grad_gate, grad_up, grad_down, *grads = finish(
        token_grad, route, grad_shared, (grad_gate, grad_up, grad_down), shared
    )
    return (
        token_grad,
        route.T,
        grad_gate[None],
        grad_up[None],
        grad_down[None],
        grads[0],
        grads[1],
        grads[2].T,
    )


def solution(mesh):
    return jax.shard_map(
        body,
        mesh=mesh,
        in_specs=(
            P("seq", "exp"),
            P("seq", "exp"),
            P("seq", None),
            P("seq", None),
            P("seq", "exp", None),
            P("seq", "exp", None),
            P("seq", "exp", None),
            P("seq", "exp"),
            P("seq", "exp"),
            P("exp", "seq"),
        ),
        out_specs=(
            P("seq", "exp"),
            P("seq", None),
            P("seq", "exp", None),
            P("seq", "exp", None),
            P("seq", "exp", None),
            P("seq", "exp"),
            P("seq", "exp"),
            P("exp", "seq"),
        ),
        check_vma=False,
    )
```

time: 250 us -> 188 us (0.75)
  Pallas kernels: 221 us -> 187 us
  other arithmetic: 10.7 us -> 0 us
  matrix products: 9.1 us -> 0 us
  local copies, waits for them, and re-layouts: 7.88 us -> 0 us
    pallas_call x3 -> x2, Pallas kernels: 221 us -> 187 us  [the longest x1 181 us: layer(): pl.pallas_call(layer_kernel, out_shape=(jax.ShapeDtypeStruct((tok_rows, w...]
    dot_general x6 -> x0, matrix products: 9.1 us -> none  [the longest x4 5.28 us: dot(): return jnp.dot(left, right, preferred_element_type=F32)]
    unnamed x17 -> x0, local copies, waits for them, and re-layouts: 5.8 us -> none
    convert_element_type x8 -> x0, other arithmetic: 4.25 us -> none  [the longest x1 1 us: body(): got_gate = got[:, MOST, :SLOT].reshape(1, experts * SLOT).astype(F32)]
where the time goes in v2:
time: 188 us
  Pallas kernels  187 us (99%)
    pallas_call x1, Pallas kernels, layer(): pl.pallas_call(layer_kernel, out_shape=(jax.ShapeDtypeStruct((tok_rows, w...  181 us
    pallas_call x1, Pallas kernels, finish(): pl.pallas_call(finish_kernel, grid=(PARTS,), out_shape=tuple((jax.ShapeDt...  6.13 us

profile of v2, /device:TPU:1, one launch (start us, length us, event | category | flops | bytes accessed | tf_op | source)
XLA Modules:
  0.0 187.9 jit_solution(3448050417923754363)
XLA Ops:
  0.6 181.0 %shard_map.161 = (bf16[128,640]{1,0:T(8,128)(2,1)}, f32[6,128]{1,0:T(8,128)}, bf16[192,5120]{1,0:T(8,128)(2,1)}, bf16[192,5120]{1,0:T(8,128)(2,1)}, bf16[192,5120]{1,0:T(8,128)(2,1)}, /*index=5*/bf16[160,640]{1,0:T(8,128)(2,1)}) custom-call(s32[6,128]{1,0:T(8,128)} %bitcast.15, bf16[6,128]{1,0:T(8,128)(2,1)} %bitcast.16, bf16[128,640]{1,0:T(8,128)(2,1)} %tok.1, ...), custom_call_target="tpu_custom_call" | custom-call | tf_op jit(solution)/shard_map/pallas_call | solution.py:635
  181.6 6.1 %shard_map.162 = (bf16[128,640]{1,0:T(8,128)(2,1)}, f32[6,128]{1,0:T(8,128)}, bf16[192,5120]{1,0:T(8,128)(2,1)}, bf16[192,5120]{1,0:T(8,128)(2,1)}, bf16[192,512...) custom-call(bf16[128,640]{1,0:T(8,128)(2,1)} %get-tuple-element.22.tok, ...), custom_call_target="tpu_custom_call" | custom-call | tf_op jit(solution)/shard_map/pallas_call | solution.py:752

commit v3 on v2

--- a/solution.py
+++ b/solution.py
@@ -12,7 +12,7 @@
 SLOT = 16
 SIDE = 4
 BLOCK = 128
-FAR = 1
+FAR = 2
 MIB = 1 << 20
 F32 = jnp.float32
 BF16 = jnp.bfloat16
@@ -87,8 +87,8 @@
             (self.seq, ring(self.exp + sign, 8)),
         )
 
-    def start(self, step):
-        for sub in range(2):
+    def start(self, step, *subs):
+        for sub in subs or range(2):
             for way in range(2):
                 if self.has(step, way, sub):
                     self.copy(step, way, sub).start()
@@ -155,6 +155,9 @@
                         self.copy(step, way, sub).wait_send()
 
 
+BANDS = ((0, 48, False, 1), (48, 32, False, -1), (80, 48, True, -1), (128, 32, True, 1))
+
+
 class Plane:
     def __init__(self):
         self.seq, self.exp, self.x, self.y, self.core = place()
@@ -164,9 +167,8 @@
         y = self.y if along_x else ring(self.y + step, SIDE)
         return ((x * SIDE + y) * 2 + self.core, self.exp)
 
-    def view(self, ref, half, wide, along_x, step):
-        count = ref.shape[3] // 2
-        rows = pl.ds(half * count, count)
+    def view(self, ref, band, wide, along_x, step):
+        rows = pl.ds(BANDS[band][0], BANDS[band][1])
         here = ring((self.x if along_x else self.y) + step, SIDE)
         if along_x:
             return ref.at[here, :, self.core, rows] if wide else ref.at[here, self.y, self.core, rows]
@@ -187,10 +189,10 @@
 def layer_kernel(
     ids, gates, tok, grad, w_gate, w_up, w_down, shared_gate, shared_up, shared_down,
     out_tok, out_route, out_gate, out_up, out_down, out_shared,
-    pick, send, got, far_send, far_got, pack, gate, xb, yb, wg, wu, wd, tx, ty, ws,
+    pick, spare, send, got, far_send, far_got, pack, gate, xb, yb, wg, wu, wd, tx, ty, ws,
     s_acc, s_dab, s_h, gp, sib, qa, qb,
     acc_a, acc_b, acc_u, da, db, hw, dat, dbt, hwt, dg,
-    pb, rp, rm, sb, sp, sm, stage, send_b, got_b,
+    pb, rp, rm, sb, sp, sm, got_b,
     own_sem, a_s, a_r, f_s, f_r, t_s, t_r, w_s, w_r, b_s, b_r, z_s, z_r, c_s, c_r, q_s, q_r,
     p_s, p_r, g_s, g_r, o_s, e_s, e_r,
 ):
@@ -237,8 +239,13 @@
     to_expert = lax.shift_right_logical(slot, 4) == lax.broadcasted_iota(jnp.int32, (slots, experts), 1)
     spread = jnp.where(to_expert, 1.0, 0.0).astype(BF16)
     slot = lax.broadcasted_iota(jnp.int32, (slots, tok_rows), 0)
-    picked = dot(spread, rank.astype(BF16)) == lax.bitwise_and(slot, SLOT - 1).astype(F32)
+    slot_rank = lax.bitwise_and(slot, SLOT - 1)
+    rank_of = dot(spread, rank.astype(BF16))
+    picked = rank_of == slot_rank.astype(F32)
     pick[...] = jnp.where(picked, 1.0, 0.0).astype(BF16)
+    for third in range(3):
+        moved = rank_of == (slot_rank - MOST + 4 * third).astype(F32)
+        spare[third] = jnp.where(moved & (slot_rank >= MOST), 1.0, 0.0).astype(BF16)
 
     units = shared_gate.shape[1]
     ws[plane.x, plane.y, core, :, :128] = shared_gate[:, :128]
@@ -290,11 +297,12 @@
 
     out_going = (send, got, a_s, a_r)
     far_going = (far_send, far_got, f_s, f_r)
+    send_b = send.at[:, : width + 128]
     home_going = (send_b, got_b, e_s, e_r)
 
-    def weight(half, phase, kind, landed):
-        along_x = half != phase
-        sign = 1 - 2 * half
+    def weight(band, phase, kind, landed):
+        along_x = BANDS[band][2] != (phase == 1)
+        sign = BANDS[band][3]
         wide = phase == 1
         if kind == 0:
             to, piece = sign, (-sign if landed else 0)
@@ -302,42 +310,37 @@
             to, piece = -sign, (sign if landed else 0)
         else:
             to, piece = sign, (2 if landed else -sign)
-        part = plane.view(ws, half, wide, along_x, piece)
+        part = plane.view(ws, band, wide, along_x, piece)
         return remote(
-            part, part, w_s.at[half, phase, kind], w_r.at[half, phase, kind], plane.device(along_x, to)
+            part, part, w_s.at[band, phase, kind], w_r.at[band, phase, kind], plane.device(along_x, to)
         )
 
-    def handed(half, phase, index, landed):
-        along_x = half != phase
-        sign = 1 - 2 * half
+    def handed(band, phase, index, landed):
+        along_x = BANDS[band][2] != (phase == 1)
+        sign = BANDS[band][3]
         wide = phase == 1
         piece = (0, -sign, sign, 2)[index]
         if landed:
             plane.core = 1 - core
-        part = plane.view(ws, half, wide, along_x, piece)
+        part = plane.view(ws, band, wide, along_x, piece)
         plane.core = core
-        return remote(part, part, b_s.at[half, phase, index], b_r.at[half, phase, index], sibling)
+        return remote(part, part, b_s.at[band, phase, index], b_r.at[band, phase, index], sibling)
 
     def weight_near(phase):
-        for half in range(2):
-            weight(half, phase, 0, True).wait_recv()
-            weight(half, phase, 2, False).start()
-            handed(half, phase, 1, False).start()
-            weight(half, phase, 1, True).wait_recv()
-            handed(half, phase, 2, False).start()
+        for band in range(4):
+            weight(band, phase, 0, True).wait_recv()
+            weight(band, phase, 2, False).start()
+            handed(band, phase, 1, False).start()
+            weight(band, phase, 1, True).wait_recv()
+            handed(band, phase, 2, False).start()
 
     def weight_far(phase):
-        for half in range(2):
-            weight(half, phase, 2, True).wait_recv()
+        for band in range(4):
+            weight(band, phase, 2, True).wait_recv()
             if phase == 0:
-                weight(half, 1, 0, False).start()
-                weight(half, 1, 1, False).start()
-            handed(half, phase, 3, False).start()
-
-    for half in range(2):
-        weight(half, 0, 0, False).start()
-        weight(half, 0, 1, False).start()
-        handed(half, 0, 0, False).start()
+                weight(band, 1, 0, False).start()
+                weight(band, 1, 1, False).start()
+            handed(band, phase, 3, False).start()
 
     send[:, :width] = dot(pick[...], tok[...]).astype(BF16)
     send[:, width : 2 * width] = dot(pick[...], grad[...]).astype(BF16)
@@ -346,6 +349,10 @@
     send[:, 2 * width :] = jnp.broadcast_to(slot_gate, (slots, 128)).astype(BF16)
 
     exchange_start(*out_going)
+    for band in range(4):
+        weight(band, 0, 0, False).start()
+        weight(band, 0, 1, False).start()
+        handed(band, 0, 0, False).start()
 
     packed = lax.broadcasted_iota(jnp.int32, pack.shape, 0)
     source = lax.broadcasted_iota(jnp.int32, pack.shape, 1)
@@ -359,13 +366,14 @@
     dg[...] = jnp.zeros_like(dg)
 
     tokens.land(1)
-    weight_near(0)
     tokens.land(2)
     exchange_end(*out_going)
+    rows = ZRing((xb.at[exp], yb.at[exp]), (xb, yb), seq, exp, z_s, z_r, 4 - FAR, FAR == 2)
     xb[exp] = dot(pack[...], got[:, :width]).astype(BF16)
+    rows.start(1, 0)
     yb[exp] = dot(pack[...], got[:, width : 2 * width]).astype(BF16)
-    rows = ZRing((xb.at[exp], yb.at[exp]), (xb, yb), seq, exp, z_s, z_r, 4 - FAR, FAR == 2)
-    rows.start(1)
+    rows.start(1, 1)
+    weight_near(0)
     weight_far(0)
     tokens.land(3)
     tokens.land(4)
@@ -373,11 +381,20 @@
     far = [(tx, xb, 4), (ty, yb, 4), (tx, xb, 3), (ty, yb, -3)][: 2 * FAR]
     for copy in own[:2]:
         copy.wait()
-    for index, (tokens_of, _, step) in enumerate(far):
-        at = slice(index * width, (index + 1) * width)
-        far_send[:, at] = dot(pick[...], tokens_of[ring(exp + step, 8)]).astype(BF16)
+    tiles = width // 128
+    spare_of, _, spare_step = far[3]
+    spare_of = spare_of[ring(exp + spare_step, 8)]
+    thirds = [dot(spare[third], spare_of) for third in range(3)]
+    for index, (tokens_of, _, step) in enumerate(far[:3]):
+        plain = dot(pick[...], tokens_of[ring(exp + step, 8)])
+        for tile in range(tiles):
+            column = index * tiles + tile
+            extra = thirds[column % 3][:, column // 3 * 128 : column // 3 * 128 + 128]
+            far_send[:, column * 128 : column * 128 + 128] = (
+                plain[:, tile * 128 : tile * 128 + 128] + extra
+            ).astype(BF16)
     exchange_start(*far_going, 1, 8)
-    gate[...] = dot(pack[...], got[:, 2 * width :])
+    gate[...] = dot(pack[...], got[:, 2 * width :]).astype(BF16)
     for copy in own[2:]:
         copy.wait()
 
@@ -397,44 +414,45 @@
         return carry
 
 
-    def landing(half, phase, kind):
-        return qb.at[half, kind] if phase else qa.at[half, kind]
-
-    def reduce_copy(half, phase, kind):
-        along_x = half == phase
-        sign = 1 - 2 * half
+    def landing(band, phase, kind):
+        size = pl.ds(0, BANDS[band][1])
+        return qb.at[band, kind, size] if phase else qa.at[band, kind, :, size]
+
+    def reduce_copy(band, phase, kind):
+        along_x = BANDS[band][2] == (phase == 1)
+        sign = BANDS[band][3]
         piece, to = ((2, sign), (-sign, -sign), (sign, sign))[kind]
         return remote(
-            plane.view(gp, half, phase == 0, along_x, piece),
-            landing(half, phase, kind),
-            q_s.at[half, phase, kind],
-            q_r.at[half, phase, kind],
+            plane.view(gp, band, phase == 0, along_x, piece),
+            landing(band, phase, kind),
+            q_s.at[band, phase, kind],
+            q_r.at[band, phase, kind],
             plane.device(along_x, to),
         )
 
-    def reduce_add(half, phase, step, kinds):
-        mine = plane.view(gp, half, phase == 0, half == phase, step)
+    def reduce_add(band, phase, step, kinds):
+        mine = plane.view(gp, band, phase == 0, BANDS[band][2] == (phase == 1), step)
         value = mine[...].astype(F32)
         for kind in kinds:
-            value += landing(half, phase, kind)[...].astype(F32)
+            value += landing(band, phase, kind)[...].astype(F32)
         mine[...] = value.astype(BF16)
 
     def reduce_start(phase):
-        for half in range(2):
-            reduce_copy(half, phase, 0).start()
-            reduce_copy(half, phase, 1).start()
+        for band in range(4):
+            reduce_copy(band, phase, 0).start()
+            reduce_copy(band, phase, 1).start()
 
     def reduce_pass(phase):
-        for half in range(2):
-            reduce_copy(half, phase, 0).wait_recv()
-            reduce_add(half, phase, 1 - 2 * half, (0,))
-            reduce_copy(half, phase, 2).start()
+        for band in range(4):
+            reduce_copy(band, phase, 0).wait_recv()
+            reduce_add(band, phase, BANDS[band][3], (0,))
+            reduce_copy(band, phase, 2).start()
 
     def reduce_end(phase):
-        for half in range(2):
-            reduce_copy(half, phase, 1).wait_recv()
-            reduce_copy(half, phase, 2).wait_recv()
-            reduce_add(half, phase, 0, (1, 2))
+        for band in range(4):
+            reduce_copy(band, phase, 1).wait_recv()
+            reduce_copy(band, phase, 2).wait_recv()
+            reduce_add(band, phase, 0, (1, 2))
 
     forward(exp)
     weight_near(1)
@@ -443,12 +461,15 @@
     exchange_start(*far_going, 17, 24)
     forward(ring(exp - 1, 8))
     forward(ring(exp + 1, 8))
+    exchange_start(*far_going, 25, 31)
+    rows.land(2)
+    forward(ring(exp - 2, 8))
+    forward(ring(exp + 2, 8))
     weight_far(1)
-    exchange_start(*far_going, 25, 31)
-    for half in range(2):
+    for band in range(4):
         for phase in range(2):
             for index in range(phase, 4):
-                handed(half, phase, index, True).wait_recv()
+                handed(band, phase, index, True).wait_recv()
 
     def shared_forward(piece, carry):
         s_acc[:, :of_x] += dot(tx[piece], weight_slice(piece, 0, of_x))
@@ -478,30 +499,22 @@
     across = remote(gp.at[:, :, 1 - core], sib, c_s, c_r, sibling)
     across.start()
 
-    rows.land(2)
-    forward(ring(exp - 2, 8))
-    forward(ring(exp + 2, 8))
-    across.wait_recv()
-
-    def add_sibling(index, carry):
-        at_x, at_y = lax.div(index, SIDE), lax.rem(index, SIDE)
-        gp[at_x, at_y, core] = (
-            gp[at_x, at_y, core].astype(F32) + sib[at_x, at_y].astype(F32)
-        ).astype(BF16)
-        return carry
-
-    lax.fori_loop(0, SIDE * SIDE, add_sibling, 0)
-    reduce_start(0)
-    lax.fori_loop(0, 8, shared_partial, 0)
-    shared_sums = ZSum(sb, (sp, sm), tok_rows // 2, seq, exp, g_s, g_r)
-    shared_sums.step(1)
     exchange_end(*far_going)
-    for index, (_, rows_of, step) in enumerate(far):
+    for index, (_, rows_of, step) in enumerate(far[:3]):
         at = slice(index * width, (index + 1) * width)
         rows_of[ring(exp + step, 8)] = dot(pack[...], far_got[:, at]).astype(BF16)
+    value = 0.0
+    for third in range(3):
+        columns = [third + 3 * tile for tile in range(tiles)]
+        part = jnp.concatenate([far_got[:, c * 128 : c * 128 + 128] for c in columns], axis=1)
+        packed = lax.broadcasted_iota(jnp.int32, pack.shape, 0)
+        source = lax.broadcasted_iota(jnp.int32, pack.shape, 1)
+        rank = lax.bitwise_and(source, SLOT - 1)
+        moved = packed == lax.shift_right_logical(source, 4) * MOST + rank - MOST + 4 * third
+        value += dot(jnp.where(moved & (rank >= MOST), 1.0, 0.0).astype(BF16), part)
+    far[3][1][ring(exp + far[3][2], 8)] = value.astype(BF16)
     forward(ring(exp + 4, 8))
     rows.land(3)
-    shared_sums.step(2)
     forward(ring(exp - 3, 8))
     forward(ring(exp + 3, 8))
 
@@ -517,7 +530,7 @@
             preferred_element_type=F32,
             precision=lax.Precision.HIGHEST,
         ).astype(BF16)
-        row_gate = gate[at, 0:1]
+        row_gate = gate[at, 0:1].astype(F32)
         scaled = row_gate * back
         grad_a = (scaled * up * slope).astype(BF16)
         grad_b = (scaled * act).astype(BF16)
@@ -533,12 +546,18 @@
     row_sums = ZSum(pb, (rp, rm), -(-pb.shape[1] // 32) * 16, seq, exp, p_s, p_r)
 
     outs = (out_gate, out_up, out_down)
+    hidden = dat.shape[0]
+
+    def stage(index, which):
+        return far_got.at[
+            index % 2 * hidden : (index % 2 + 1) * hidden, which * width : (which + 1) * width
+        ]
 
     def out_copy(index, which):
         piece = ring(exp + index, 8)
         cols = pl.ds(pl.multiple_of(piece * width, 128), width)
         return pltpu.make_async_copy(
-            stage.at[index % 2, which], outs[which].at[:, cols], o_s.at[index % 2, which]
+            stage(index, which), outs[which].at[:, cols], o_s.at[index % 2, which]
         )
 
     def weight_grads(index):
@@ -546,59 +565,73 @@
         if index >= 2:
             for which in range(3):
                 out_copy(index - 2, which).wait()
-        stage[index % 2, 0] = dot(dat[...], xb[piece]).astype(BF16)
-        stage[index % 2, 1] = dot(dbt[...], xb[piece]).astype(BF16)
-        stage[index % 2, 2] = dot(hwt[...], yb[piece]).astype(BF16)
+        stage(index, 0)[...] = dot(dat[...], xb[piece]).astype(BF16)
+        stage(index, 1)[...] = dot(dbt[...], xb[piece]).astype(BF16)
+        stage(index, 2)[...] = dot(hwt[...], yb[piece]).astype(BF16)
         for which in range(3):
             out_copy(index, which).start()
 
     partial(ring(exp + 4, 8))
     row_sums.step(1)
+    lax.fori_loop(0, 8, shared_partial, 0)
+    shared_sums = ZSum(sb, (sp, sm), tok_rows // 2, seq, exp, g_s, g_r)
+    shared_sums.step(1)
     partial(ring(exp + 3, 8))
     partial(ring(exp - 3, 8))
     row_sums.step(2)
-    reduce_pass(0)
+
+    def add_sibling(index, carry):
+        at_x, at_y = lax.div(index, SIDE), lax.rem(index, SIDE)
+        gp[at_x, at_y, core] = (
+            gp[at_x, at_y, core].astype(F32) + sib[at_x, at_y].astype(F32)
+        ).astype(BF16)
+        return carry
+
+    across.wait_recv()
+    lax.fori_loop(0, SIDE * SIDE, add_sibling, 0)
+    reduce_start(0)
     partial(ring(exp + 2, 8))
     partial(ring(exp - 2, 8))
     weight_grads(0)
     row_sums.step(3)
-    reduce_end(0)
-    reduce_start(1)
+    shared_sums.step(2)
     partial(ring(exp + 1, 8))
     partial(ring(exp - 1, 8))
     weight_grads(1)
     weight_grads(2)
-    weight_grads(3)
+    reduce_pass(0)
     row_sums.step(4)
     shared_sums.step(3)
-    reduce_pass(1)
     partial(exp)
-    for index in range(4, 8):
+    for index in range(3, 8):
         weight_grads(index)
+    reduce_end(0)
+    reduce_start(1)
     whole = row_sums.total()
 
+    exchange_sent(*out_going)
     send_b[:, :width] = dot_rows(pack[...], whole[:count].astype(BF16)).astype(BF16)
     route = whole[count : count + 16, :count].T[:, 0:1]
     route = jnp.broadcast_to(route, (count, 128)).astype(BF16)
     send_b[:, width:] = dot_rows(pack[...], route).astype(BF16)
     exchange_start(*home_going)
     shared_sums.step(4)
+    reduce_pass(1)
 
     tokens.finish()
     rows.finish()
     row_sums.finish()
     reduce_end(1)
     out_shared[...] = gp[plane.x, plane.y, core]
-    exchange_sent(*out_going)
     exchange_sent(*far_going)
     across.wait_send()
-    for half in range(2):
+    for band in range(4):
         for phase in range(2):
             for kind in range(3):
-                weight(half, phase, kind, False).wait_send()
-                reduce_copy(half, phase, kind).wait_send()
+                weight(band, phase, kind, False).wait_send()
+                reduce_copy(band, phase, kind).wait_send()
             for index in range(phase, 4):
-                handed(half, phase, index, False).wait_send()
+                handed(band, phase, index, False).wait_send()
     for index in (6, 7):
         for which in range(3):
             out_copy(index, which).wait()
@@ -646,12 +679,13 @@
         out_specs=vmem_specs(2) + any_specs(3) + vmem_specs(1),
         scratch_shapes=[
             vmem((slots, tok_rows), BF16),
+            vmem((3, slots, tok_rows), BF16),
             vmem((slots, 2 * width + 128), BF16),
             vmem((slots, 2 * width + 128), BF16),
-            vmem((slots, 2 * FAR * width), BF16),
-            vmem((slots, 2 * FAR * width), BF16),
+            vmem((slots, 3 * width), BF16),
+            vmem((slots, 3 * width), BF16),
             vmem((count, slots), BF16),
-            vmem((count, 128), F32),
+            vmem((count, 128), BF16),
             vmem((8, count, width), BF16),
             vmem((8, count, width), BF16),
             vmem((hidden, model), BF16),
@@ -665,8 +699,8 @@
             vmem((tok_rows, lanes - of_x), BF16),
             vmem((SIDE, SIDE, 2, chunk, lanes), BF16),
             vmem((SIDE, SIDE, chunk, lanes), BF16),
-            vmem((2, 3, SIDE, chunk // 2, lanes), BF16),
-            vmem((2, 3, chunk // 2, lanes), BF16),
+            vmem((4, 3, SIDE, 48, lanes), BF16),
+            vmem((4, 3, 48, lanes), BF16),
             vmem((count, hidden), F32),
             vmem((count, hidden), F32),
             vmem((count, hidden), F32),
@@ -683,8 +717,6 @@
             vmem((8, tok_rows, width), BF16),
             vmem((4, tok_rows, width), BF16),
             vmem((4, tok_rows, width), BF16),
-            vmem((2, 3, hidden, width), BF16),
-            vmem((slots, width + 128), BF16),
             vmem((slots, width + 128), BF16),
             dma((5,)),
             dma((31,)),
@@ -693,16 +725,16 @@
             dma((31,)),
             dma((2, 2, 4)),
             dma((2, 2, 4)),
-            dma((2, 2, 3)),
-            dma((2, 2, 3)),
-            dma((2, 2, 4)),
-            dma((2, 2, 4)),
+            dma((4, 2, 3)),
+            dma((4, 2, 3)),
+            dma((4, 2, 4)),
+            dma((4, 2, 4)),
             dma((2, 2, 4)),
             dma((2, 2, 4)),
             dma,
             dma,
-            dma((2, 2, 3)),
-            dma((2, 2, 3)),
+            dma((4, 2, 3)),
+            dma((4, 2, 3)),
             dma((2, 2, 4)),
             dma((2, 2, 4)),
             dma((2, 2, 4)),
@@ -717,7 +749,7 @@
     )(ids, gates, tok, grad, w_gate, w_up, w_down, shared_gate, shared_up, shared_down)
 
 
-PARTS = 4
+PARTS = 2
 
 
 def finish_kernel(

time: 188 us -> 181 us (0.963)
  Pallas kernels: 187 us -> 180 us
    pallas_call x1, Pallas kernels: 181 us -> 175 us  [layer(): pl.pallas_call(layer_kernel, out_shape=(jax.ShapeDtypeStruct((tok_rows, w...]
where the time goes in v3:
time: 181 us
  Pallas kernels  180 us (99%)
    pallas_call x1, Pallas kernels, layer(): pl.pallas_call(layer_kernel, out_shape=(jax.ShapeDtypeStruct((tok_rows, w...  175 us
    pallas_call x1, Pallas kernels, finish(): pl.pallas_call(finish_kernel, grid=(PARTS,), out_shape=tuple((jax.ShapeDt...  5.22 us

profile of v3, /device:TPU:1, one launch (start us, length us, event | category | flops | bytes accessed | tf_op | source)
XLA Modules:
  0.0 180.8 jit_solution(9599198431307193371)
XLA Ops:
  0.6 174.8 %shard_map.161 = (bf16[128,640]{1,0:T(8,128)(2,1)}, f32[6,128]{1,0:T(8,128)}, bf16[192,5120]{1,0:T(8,128)(2,1)}, bf16[192,5120]{1,0:T(8,128)(2,1)}, bf16[192,5120]{1,0:T(8,128)(2,1)}, /*index=5*/bf16[160,640]{1,0:T(8,128)(2,1)}) custom-call(s32[6,128]{1,0:T(8,128)} %bitcast.15, bf16[6,128]{1,0:T(8,128)(2,1)} %bitcast.16, bf16[128,640]{1,0:T(8,128)(2,1)} %tok.1, ...), custom_call_target="tpu_custom_call" | custom-call | tf_op jit(solution)/shard_map/pallas_call | solution.py:668
  175.4 5.2 %shard_map.162 = (bf16[128,640]{1,0:T(8,128)(2,1)}, f32[6,128]{1,0:T(8,128)}, bf16[192,5120]{1,0:T(8,128)(2,1)}, bf16[192,5120]{1,0:T(8,128)(2,1)}, bf16[192,512...) custom-call(bf16[128,640]{1,0:T(8,128)(2,1)} %get-tuple-element.22.tok, ...), custom_call_target="tpu_custom_call" | custom-call | tf_op jit(solution)/shard_map/pallas_call | solution.py:784
